TPU v7x, 32 devices: a whole 2x2x4 slice. The times are simulated.
32 devices in a mesh: sens: 4 (over y, core), par: 8 (over z, x).
Axes of the slice: x: 2, y: 2, z: 4, core: 2. Of those that a mesh axis runs over, the one named last changes fastest.
Arguments:
- data: bfloat16 [32, 600, 420], P(None, 'sens'), may hold values from -6 to 6
- green: bfloat16 [64, 600, 2, 1024], P(None, 'sens', None, 'par'), may hold values from -0.1875 to 0.1875
- freqs: int32 [64], replicated, may hold values from 1 to 209, as said below
- sensor_order: int32 [600], P('sens'), may hold values from 0 to 599, each once
- kappa: float32 [8, 128], P('par'), may hold values from 0.05 to 0.5
- theta: float32 [8, 128], P('par'), may hold values from 0.5 to 2
Outputs:
- prior_field: bfloat16 [32, 420, 8, 128], P('sens', None, 'par')
Inputs may be any that keep to these rules, and one draw needn't show every extreme that they name: `freqs`: distinct; both 1 and 209 appear. `sensor_order`: each sensor fills exactly one slot.
All inputs are finite; a program needn't handle non-finite values.
Results may differ from a plain program's by a relative error of at most 0.015.
Values may be sent and summed in bfloat16 or wider, within the bound.
A program may use at most 64 MiB of HBM per device.

v0:
```python
import math

import jax
import jax.numpy as jnp
from jax import lax
from jax.sharding import PartitionSpec as P

NT = 420
K = 64
COLS = 128
SWEEPS = 6


lower_bound = 0.05
upper_bound = 16.5


def make_tables(freqs):
    times = jnp.arange(NT, dtype=jnp.int32)
    phase = times[:, None] * freqs[None, :] % NT
    angle = phase.astype(jnp.float32) * (2.0 * math.pi / NT)
    cosine = jnp.cos(angle)
    sine = jnp.sin(angle)
    forward = (jnp.concatenate([cosine, -sine], axis=1) / math.sqrt(NT)).astype(jnp.bfloat16)
    inverse = (jnp.concatenate([cosine, -sine], axis=1) / math.sqrt(K)).astype(jnp.bfloat16)
    return (forward, inverse)


def chebyshev_scalars():
    center = 0.5 * (upper_bound + lower_bound)
    radius = 0.5 * (upper_bound - lower_bound)
    alphas = []
    betas = []
    alpha = 1.0 / center
    for sweep_index in range(SWEEPS):
        if sweep_index == 0:
            alpha = 1.0 / center
            beta = 0.0
        else:
            if sweep_index == 1:
                beta = 0.5 * (radius * alpha) ** 2
            else:
                beta = (radius * alpha / 2.0) ** 2
            alpha = 1.0 / (center - beta / alpha)
        alphas.append(alpha)
        betas.append(beta)
    return (alphas, betas)


def run_sweeps(grid, operator):
    alphas, betas = chebyshev_scalars()
    solution = jnp.zeros_like(grid)
    residual = grid
    direction = grid
    for sweep_index in range(SWEEPS):
        if sweep_index == 0:
            direction = residual
        else:
            direction = residual + betas[sweep_index] * direction
        solution = solution + alphas[sweep_index] * direction
        if sweep_index + 1 < SWEEPS:
            residual = residual - alphas[sweep_index] * operator(direction)
    return solution


def local(data, green, freqs, sensor_order, kappa, theta):
    probes, sensors_here, steps_count = data.shape
    forward, inverse = make_tables(freqs)
    spectra_local = jnp.einsum(
        "rst,tj->rsj", data, forward, preferred_element_type=jnp.float32
    ).astype(jnp.bfloat16)
    spectra_all = lax.all_gather(spectra_local, "sens", axis=1, tiled=True)
    slotted = jnp.take(spectra_all, sensor_order, axis=1)
    cells_here = green.shape[-1]
    left_side = jnp.transpose(slotted.reshape(probes, sensors_here, 2, K), (3, 2, 0, 1))
    left_side = left_side.reshape(K, 2 * probes, sensors_here)
    right_side = green.reshape(K, sensors_here, 2 * cells_here)
    products = lax.dot_general(
        left_side, right_side, (((2,), (1,)), ((0,), (0,))), preferred_element_type=jnp.float32
    )
    products = products.reshape(K, 2, probes, 2, cells_here)
    real_part = products[:, 0, :, 0, :] + products[:, 1, :, 1, :]
    imag_part = products[:, 1, :, 0, :] - products[:, 0, :, 1, :]
    partial_sum = jnp.transpose(jnp.concatenate([real_part, imag_part], axis=0), (1, 0, 2))
    sens_count = lax.axis_size("sens")
    probes_here = probes // sens_count
    total = lax.psum(partial_sum.astype(jnp.bfloat16), "sens").astype(jnp.float32)
    adjoint = lax.dynamic_slice_in_dim(total, lax.axis_index("sens") * probes_here, probes_here, 0)
    adjoint_b = adjoint.astype(jnp.bfloat16)
    par_count = lax.axis_size("par")
    col_groups = COLS // par_count
    rows_all = cells_here // col_groups
    rows_here = rows_all // par_count
    field = jnp.einsum("tj,rjp->rtp", inverse, adjoint_b, preferred_element_type=jnp.float32)
    groups = probes_here * NT
    moved = lax.all_to_all(
        field.reshape(groups, rows_all, col_groups, 1).astype(jnp.bfloat16),
        "par",
        split_axis=0,
        concat_axis=3,
        tiled=True,
    ).astype(jnp.float32)
    fields_here = moved.reshape(groups // par_count, rows_all, COLS)
    kappa_all, theta_all = (
        lax.all_gather(kappa, "par", axis=0, tiled=True),
        lax.all_gather(theta, "par", axis=0, tiled=True),
    )
    theta_full = jnp.pad(theta_all, 1, mode="edge")
    north = 0.5 * (theta_all + theta_full[:-2, 1:-1])
    south = 0.5 * (theta_all + theta_full[2:, 1:-1])
    west = 0.5 * (theta_all + theta_full[1:-1, :-2])
    east = 0.5 * (theta_all + theta_full[1:-1, 2:])
    diagonal = kappa_all + north + south + west + east

    def whole_operator(field_in):
        padded = jnp.pad(field_in, ((0, 0), (1, 1), (1, 1)))
        return (
            diagonal * field_in
            - north * padded[:, :-2, 1:-1]
            - south * padded[:, 2:, 1:-1]
            - west * padded[:, 1:-1, :-2]
            - east * padded[:, 1:-1, 2:]
        )

    solution = run_sweeps(fields_here, whole_operator).astype(jnp.bfloat16)
    back = lax.all_to_all(solution, "par", split_axis=1, concat_axis=0, tiled=True)
    return back.reshape(probes_here, NT, rows_here, COLS)


def solution(mesh):
    placed = (
        P(None, "sens", None),
        P(None, "sens", None, "par"),
        P(),
        P("sens"),
        P("par", None),
        P("par", None),
    )
    return jax.shard_map(
        local, mesh=mesh, in_specs=placed, out_specs=P("sens", None, "par", None), check_vma=False
    )
```

profile of v0, /device:TPU:0, one launch (start us, length us, event | category | flops | bytes accessed | tf_op | source)
XLA Modules:
  0.0 259.0 jit_solution(11339626209574285668)
XLA Ops:
  6.5 1.6 fusion.73
  8.1 7.6 %fusion.60 = bf16[32,150,128]{2,1,0:T(8,128)(2,1)S(1)} fusion(bf16[32,150,420]{2,0,1:T(8,128)(2,1)} %param.6, f32[420,64]{1,0:T(8,128)S(1)} %get-tuple-element.27, f32[420,64]{1,0:T(8,128)S(1)} %get-tuple-element.26), kind=kOutput, calls=%fused_computation.85 | convolution fusion | flops 516871680 | bytes 5475840 | tf_op jit(solution)/shard_map/rst,tj->rsj/dot_general | solution.py:69
  15.7 1.2 copy.39
  17.0 0.2 all-reduce.7.cloned.1.call-start
  17.2 11.7 %reshape.70 = bf16[64,150,256]{2,1,0:T(8,128)(2,1)} reshape(bf16[64,150,2,128]{3,2,1,0:T(2,128)(2,1)} %param.7) | data formatting | bytes 9830400 | tf_op jit(solution)/shard_map/reshape | solution.py:77
  28.9 29.5 %all-gather.4.cloned.1.call-done = bf16[32,600,128]{2,0,1:T(8,128)(2,1)} async-done(((bf16[32,150,128]{2,0,1:T(8,128)(2,1)}), bf16[32,600,128]{2,0,1:T(8,128)(2,1)}) %all-gather.4.cloned.1.call-update) | async-done | bytes 4915216 | tf_op jit(solution)/shard_map/all_gather | solution.py:72
  58.4 4.2 %gather_fusion = bf16[150,32,128]{2,1,0:T(8,128)(2,1)} fusion(bf16[32,600,128]{2,0,1:T(8,128)(2,1)} %all-gather.4.cloned.1.call-done, s32[1024]{0:T(1024)S(1)} %pad_clamp_fusion), kind=kCustom, calls=%fused_computation | custom fusion | bytes 2458200 | tf_op jit(solution)/shard_map/jit(_take)/gather | solution.py:73
  62.6 4.3 %gather.7 = bf16[32,150,2,64]{3,2,0,1:T(2,128)(2,1)S(1)} reshape(bf16[32,150,128]{2,0,1:T(8,128)(2,1)} %bitcast.48) | data formatting | bytes 2457600 | tf_op jit(solution)/shard_map/jit(_take)/gather | solution.py:73
  67.0 3.9 %fusion.2 = bf16[64,2,32,150]{0,1,2,3:T(2,128)(2,1)} fusion(bf16[32,150,2,64]{3,2,0,1:T(2,128)(2,1)S(1)} %gather.7, pred[150]{0:T(512)(128)(4,1)S(1)} %compare_and_fusion), kind=kLoop, calls=%fused_computation.24 | loop fusion | flops 614400 | bytes 2457750 | tf_op jit(solution)/shard_map/transpose | solution.py:75
  70.9 7.4 %copy.40 = bf16[64,2,32,150]{3,2,1,0:T(8,128)(2,1)S(1)} copy(bf16[64,2,32,150]{0,1,2,3:T(2,128)(2,1)} %fusion.2) | data formatting | bytes 2457600 | tf_op jit(solution)/shard_map/transpose | solution.py:75
  78.3 5.3 %fusion.104 = f32[64,64,256]{2,1,0:T(8,128)} fusion(bf16[64,64,150]{2,1,0:T(8,128)(2,1)S(1)} %bitcast.47, bf16[64,150,256]{2,1,0:T(8,128)(2,1)} %reshape.70), kind=kOutput, calls=%fused_computation.142 | convolution fusion | flops 314572800 | bytes 10338304 | tf_op jit(solution)/shard_map/dot_general | solution.py:78
  83.6 5.8 %reshape.50 = f32[64,2,32,2,128]{4,3,2,1,0:T(2,128)} reshape(f32[64,64,256]{2,1,0:T(8,128)} %fusion.104) | data formatting | bytes 8388608 | tf_op jit(solution)/shard_map/reshape | solution.py:81
  89.3 7.7 %fusion.102 = (f32[64,1,32,1,128]{4,3,2,1,0:T(1,128)S(1)}, f32[64,1,32,1,128]{4,3,2,1,0:T(1,128)S(1)}, f32[64,1,32,1,128]{4,3,2,1,0:T(1,128)S(1)}, f32[64,1,32,1,128]{4,3,2,1,0:T(1,128)S(1)}) fusion(f32[64,2,32,2,128]{4,3,2,1,0:T(2,128)} %reshape.50), kind=kLoop, calls=%fused_computation.140 | loop fusion | bytes 8388608 | tf_op jit(solution)/shard_map/slice | solution.py:82
  97.0 2.3 fusion.66
  99.3 1.1 maximum_bitcast_fusion
  100.4 36.3 %all-reduce.7.cloned.1.call-done = bf16[32,128,128]{2,1,0:T(8,128)(2,1)} async-done(((bf16[32,128,128]{2,1,0:T(8,128)(2,1)}), bf16[32,128,128]{2,1,0:T(8,128)(2,1)}) %all-reduce.7.cloned.1.call-update) | async-done | bytes 1048592 | tf_op jit(solution)/shard_map/psum | solution.py:87
  136.7 1.4 fusion.63
  138.1 5.8 %reshape.71 = bf16[3360,8,16,1]{2,1,3,0:T(8,128)(2,1)} reshape(bf16[8,420,128]{2,1,0:T(8,128)(2,1)S(1)} %fusion.63) | data formatting | bytes 1720320 | tf_op jit(solution)/shard_map/convert_element_type | solution.py:97
  143.9 10.1 %reshape.72 = bf16[8,2,26880]{2,1,0:T(2,128)(2,1)} reshape(bf16[3360,1,8,16]{3,2,1,0:T(8,128)(2,1)} %bitcast.45) | data formatting | bytes 1720320
  154.0 5.5 %all-to-all-start = ((bf16[8,2,26880]{2,1,0:T(2,128)(2,1)}), bf16[8,2,26880]{2,1,0:T(2,128)(2,1)S(1)}, u32[]{:S(2)}, u32[]{:S(2)}) async-start(bf16[8,2,26880]{2,1,0:T(2,128)(2,1)} %reshape.72), calls=%async_computation | async-start | bytes 1720320 | tf_op jit(solution)/shard_map/all_to_all | solution.py:96
  159.5 28.0 %all-gather.1 = f32[8,1,128]{2,1,0:T(1,128)S(1)} all-gather(f32[1,1,128]{2,1,0:T(1,128)S(1)} %bitcast.53), channel_id=1, replica_groups=mesh['sens'=4,'par'=8] {'par'}, dimensions={0}, use_global_device_ids=true | all-gather | bytes 4608 | tf_op jit(solution)/shard_map/all_gather | solution.py:106
  187.5 19.7 %all-gather = f32[8,1,128]{2,1,0:T(1,128)S(1)} all-gather(f32[1,1,128]{2,1,0:T(1,128)S(1)} %bitcast.54), channel_id=1, replica_groups=mesh['sens'=4,'par'=8] {'par'}, dimensions={0}, use_global_device_ids=true | all-gather | bytes 4608 | tf_op jit(solution)/shard_map/all_gather | solution.py:105
  207.4 7.5 %reshape.73 = bf16[3360,1,8,16]{3,2,1,0:T(8,128)(2,1)} reshape(bf16[8,2,26880]{2,1,0:T(2,128)(2,1)S(1)} %all-to-all-done) | data formatting | bytes 1720320
  214.9 7.4 %copy.49 = f32[8,420,8,16,1]{1,0,3,2,4:T(8,128)S(1)} copy(bf16[8,420,8,16,1]{3,2,1,0,4:T(8,128)(2,1)} %bitcast.46) | data formatting | bytes 2580480 | tf_op jit(solution)/shard_map/convert_element_type | solution.py:102
  222.4 1.7 multiply_add_fusion.3
  224.1 1.7 multiply_add_fusion.2
  225.8 1.7 multiply_add_fusion.1
  227.6 1.7 multiply_add_fusion
  229.3 2.5 fusion.53
  231.9 0.6 copy.50
  232.5 18.7 %all_to_all.24 = bf16[420,8,128]{2,0,1:T(8,128)(2,1)S(1)} all-to-all(bf16[420,8,128]{2,0,1:T(8,128)(2,1)S(1)} %copy.50), channel_id=1, replica_groups=mesh['sens'=4,'par'=8] {'par'}, dimensions={1} | all-to-all | bytes 1720320 | tf_op jit(solution)/shard_map/all_to_all | solution.py:126
  251.2 1.0 copy.51
  (17 shorter events, 0.2 us)
Async XLA Ops:
  6.5 51.9 %all-gather.4.cloned.1.call-start = ((), (), s32[]{:S(2)}) async-start(), calls=%async_computation.2 | async-start | bytes 6144000 | tf_op jit(solution)/shard_map/all_gather | solution.py:72
  17.0 11.9 %copy-start = (s32[150]{0:T(256)S(1)}, s32[150]{0:T(256)}, u32[]{:S(2)}) copy-start(s32[150]{0:T(256)} %param.9) | copy-start | bytes 1804
  17.0 119.7 %all-reduce.7.cloned.1.call-start = ((), (), s32[]{:S(2)}) async-start(), calls=%async_computation.3 | async-start | bytes 2097152 | tf_op jit(solution)/shard_map/psum | solution.py:87
  143.9 15.6 %copy-start.1 = (f32[1,128]{1,0:T(1,128)S(1)}, f32[1,128]{1,0:T(1,128)}, u32[]{:S(2)}) copy-start(f32[1,128]{1,0:T(1,128)} %param.11) | copy-start | bytes 1540
  143.9 43.6 %copy-start.2 = (f32[1,128]{1,0:T(1,128)S(1)}, f32[1,128]{1,0:T(1,128)}, u32[]{:S(2)}) copy-start(f32[1,128]{1,0:T(1,128)} %param.10) | copy-start | bytes 1540
  154.0 53.4 %all-to-all-start = ((bf16[8,2,26880]{2,1,0:T(2,128)(2,1)}), bf16[8,2,26880]{2,1,0:T(2,128)(2,1)S(1)}, u32[]{:S(2)}, u32[]{:S(2)}) async-start(bf16[8,2,26880]{2,1,0:T(2,128)(2,1)} %reshape.72), calls=%async_computation | async-start | bytes 1720320 | tf_op jit(solution)/shard_map/all_to_all | solution.py:96
Sparse Core Ops, SparseCore 0:
  17.1 41.2 all-gather.3
  100.5 36.1 all-reduce.6
where the time goes:
time: 260 us; the launch traced here: 259 us
  local copies, waits for them, and re-layouts  74.9 us (29%)
  blocking collectives  66.4 us (26%)
  waiting for transfers between devices  65.8 us (25%)
  other arithmetic  18.4 us (7%)
  matrix products  14.2 us (5%)
  between operations  13.5 us (5%)
  starting transfers between devices  5.73 us (2%)
    psum x1, waiting for transfers between devices, local(): lax.psum(partial_sum.astype(jnp.bfloat16), 'sens').astype(jnp.float32)  36.3 us
    all_gather x1, waiting for transfers between devices, local(): spectra_all = lax.all_gather(spectra_local, 'sens', axis=1, tiled=True)  29.5 us
    all_gather x1, blocking collectives, local(): lax.all_gather(theta, 'par', axis=0, tiled=True)  28 us
    all_gather x1, blocking collectives, local(): lax.all_gather(kappa, 'par', axis=0, tiled=True)  19.7 us
    all_to_all x1, blocking collectives, local(): lax.all_to_all(solution, 'par', split_axis=1, concat_axis=0, tiled=True)  18.7 us
    unnamed x8, local copies, waits for them, and re-layouts  17.6 us
    reshape x1, local copies, waits for them, and re-layouts, local(): right_side = green.reshape(K, sensors_here, 2 * cells_here)  11.7 us
    gather x2, local copies, waits for them, and re-layouts, local(): slotted = jnp.take(spectra_all, sensor_order, axis=1)  8.57 us
  transfers between devices with their start and end apart: 3, of which 2 were waited for; matrix products, arithmetic and copies ran while one was open for 5% of the time, Pallas kernels for 0%

commit v1 on v0

v1 whole, which is shorter than its diff:
```python
import functools
import math

import jax
import jax.numpy as jnp
from jax import lax
from jax.experimental import pallas as pl
from jax.experimental.pallas import tpu as pltpu
from jax.sharding import PartitionSpec as P

NT = 420
SWEEPS = 6
lower_bound = 0.05
upper_bound = 16.5
MESH = pl.DeviceIdType.MESH
F32 = jnp.float32
BF16 = jnp.bfloat16


def chebyshev_scalars():
    center = 0.5 * (upper_bound + lower_bound)
    radius = 0.5 * (upper_bound - lower_bound)
    alphas = []
    betas = []
    alpha = 1.0 / center
    for sweep_index in range(SWEEPS):
        if sweep_index == 0:
            alpha = 1.0 / center
            beta = 0.0
        else:
            if sweep_index == 1:
                beta = 0.5 * (radius * alpha) ** 2
            else:
                beta = (radius * alpha / 2.0) ** 2
            alpha = 1.0 / (center - beta / alpha)
        alphas.append(alpha)
        betas.append(beta)
    return (alphas, betas)


def iota(shape, dim):
    return lax.broadcasted_iota(jnp.int32, shape, dim)


def round_up(value, unit):
    return -(-value // unit) * unit


def kernel(
    n_sens, n_par, probes, sensors, kper,
    data_hbm, green_hbm, wf, wi, order, kappa, theta,
    out,
    data_v, green_v, green_f, green_s, spec_f, ubuf, vbuf, vt, part, rsbuf, adj, gin,
    coef, ysend, sin, sf,
    load_sem, u_send, u_recv, z_send, z_recv, x_send, x_recv, rs_send, rs_recv,
    a_send, a_recv, c_send, c_recv, y_send, y_recv,
):
    a = lax.axis_index("sens")
    b = lax.axis_index("par")
    nz = n_par // 2
    zpos = b // 2
    xpos = b % 2
    here = probes // n_sens
    lanes = here * 2 * kper
    fields = kper * 2 * here
    spad = ubuf.shape[1]
    groups = n_sens
    width = out.shape[-1]
    cg = width // n_par

    def sens_peer(e):
        return {"sens": (a + e) % n_sens}

    def par_peer(e):
        return {"par": (b + e) % n_par}

    barrier = pltpu.get_barrier_semaphore()
    for e in range(1, n_sens):
        pl.semaphore_signal(barrier, inc=1, device_id=sens_peer(e), device_id_type=MESH)
    for e in range(1, n_par):
        pl.semaphore_signal(barrier, inc=1, device_id=par_peer(e), device_id_type=MESH)

    chunks = data_v.shape[0]
    loads = []
    for c in range(chunks):
        load = pltpu.make_async_copy(data_hbm.at[c], data_v.at[c], load_sem.at[c])
        load.start()
        loads.append(load)
    green_load = pltpu.make_async_copy(green_hbm, green_v, load_sem.at[chunks])
    green_load.start()

    pick = (iota((width, width), 0) // n_par + b * cg == iota((width, width), 1)).astype(F32)
    own = iota((n_par, width), 1) % n_par == iota((n_par, width), 0)
    for index, ref in enumerate((kappa, theta)):
        spread = jnp.where(own, jnp.broadcast_to(ref[...], (n_par, width)), 0.0)
        coef[0, index] = jnp.dot(spread, pick, precision=lax.Precision.HIGHEST, preferred_element_type=F32)

    rows = data_v.shape[1]
    wide = wf.shape[1]
    keep = iota((rows // here, here, wide), 2) // (2 * kper) == iota((rows // here, here, wide), 1)
    for c in range(chunks):
        loads[c].wait()
        prod = jnp.dot(data_v[c], wf[...], preferred_element_type=F32)
        prod = jnp.where(keep, prod.reshape(rows // here, here, wide), 0.0)
        spec_f[c * (rows // here):(c + 1) * (rows // here), :] = jnp.sum(prod, axis=1)
    ubuf[0, spad - 16:, :] = jnp.zeros((16, groups * lanes), BF16)
    for g in range(groups):
        ubuf[0, :sensors, g * lanes:(g + 1) * lanes] = spec_f[pl.ds(g, sensors, stride=groups), :][:, :lanes].astype(BF16)

    pl.semaphore_wait(barrier, n_sens + n_par - 2)
    sends = []

    def push(src, dst, ssem, rsem, peer):
        copy = pltpu.make_async_remote_copy(
            src_ref=src, dst_ref=dst, send_sem=ssem, recv_sem=rsem, device_id=peer, device_id_type=MESH
        )
        copy.start()
        sends.append(copy)
        return copy

    u_copies = [push(ubuf.at[0], ubuf.at[e], u_send.at[e], u_recv.at[e], sens_peer(e)) for e in range(1, n_sens)]
    c_copies = [push(coef.at[0], coef.at[e], c_send.at[e], c_recv.at[e], par_peer(e)) for e in range(1, n_par)]

    green_load.wait()
    green_s[:, spad - 16:, :] = jnp.zeros((green_s.shape[0], 16, green_s.shape[2]), BF16)

    def split(block, carry):
        green_f[...] = green_v[block].astype(F32)
        for k in range(kper):
            for c in range(2):
                piece = green_f[pl.ds(k * 2 * sensors + c, sensors, stride=2), :]
                green_s[block * kper + k, :sensors, c * width:(c + 1) * width] = piece.astype(BF16)
        return carry

    lax.fori_loop(0, n_par, split, 0)

    picked = jnp.zeros((spad, groups * lanes), F32)
    wanted = jnp.broadcast_to(order[...], (spad, spad))
    for e in range(n_sens):
        if e:
            u_copies[e - 1].wait_recv()
        base = ((a - e + n_sens) % n_sens) * sensors
        position = iota((spad, spad), 1)
        match = ((wanted == position + base) & (position < sensors)).astype(F32).astype(BF16)
        picked = picked + jnp.dot(match, ubuf[e], preferred_element_type=F32)
    vbuf[0, 0] = picked.astype(BF16)

    partner = {"par": zpos * 2 + (1 - xpos)}
    z_copies = {}
    x_copies = {}
    for d in range(1, nz):
        peer = {"par": ((zpos + d) % nz) * 2 + xpos}
        z_copies[d] = push(vbuf.at[0, 0], vbuf.at[d, 0], z_send.at[d], z_recv.at[d], peer)
    x_copies[0] = push(vbuf.at[0, 0], vbuf.at[0, 1], x_send.at[0], x_recv.at[0], partner)

    rs_copies = {}
    a_copies = []
    steps = [(d, xi) for d in range(nz) for xi in range(2)]

    def owner(step):
        d, xi = step
        other = xpos if xi == 0 else 1 - xpos
        return ((zpos - d + nz) % nz) * 2 + other

    def products(index):
        d, xi = steps[index]
        if xi:
            x_copies[d].wait_recv()
        elif d:
            z_copies[d].wait_recv()
            x_copies[d] = push(vbuf.at[d, 0], vbuf.at[d, 1], x_send.at[d], x_recv.at[d], partner)
        block = owner(steps[index])
        for t in range(vt.shape[0]):
            size = min(spad - t * 128, 128)
            vt[t, :, :size] = jnp.transpose(vbuf[d, xi, t * 128:t * 128 + size, :].astype(F32))
        half = probes
        for k in range(kper):
            left = []
            for t in range(vt.shape[0]):
                real = vt[t, pl.ds(k, half, stride=2 * kper), :]
                imag = vt[t, pl.ds(kper + k, half, stride=2 * kper), :]
                left.append(jnp.concatenate([real, imag], axis=0).astype(BF16)[:, :min(spad - t * 128, 128)])
            left = jnp.concatenate(left, axis=1)
            prod = jnp.dot(left, green_s[block * kper + k], preferred_element_type=F32)
            re = prod[:half, :width] + prod[half:, width:]
            im = prod[half:, :width] - prod[:half, width:]
            for g in range(groups):
                both = jnp.concatenate([re[g * here:(g + 1) * here], im[g * here:(g + 1) * here]], axis=0)
                part[index, g, k * 2 * here:(k + 1) * 2 * here, :] = both.astype(BF16)
        rs_copies[index] = [
            push(
                part.at[index, (a + e) % n_sens], rsbuf.at[index, e - 1],
                rs_send.at[index, e - 1], rs_recv.at[index, e - 1], sens_peer(e),
            )
            for e in range(1, n_sens)
        ]

    def reduce(index):
        for copy in rs_copies[index]:
            copy.wait_recv()
        total = part[index, a].astype(F32)
        for e in range(1, n_sens):
            total = total + rsbuf[index, e - 1].astype(F32)
        if index == 0:
            gin[b] = total.astype(BF16)
        else:
            adj[index] = total.astype(BF16)
            a_copies.append(
                push(adj.at[index], gin.at[b], a_send.at[index], a_recv.at[index], {"par": owner(steps[index])})
            )

    for index in range(n_par):
        products(index)
        if index:
            reduce(index - 1)
    reduce(n_par - 1)

    for copy in c_copies:
        copy.wait_recv()
    kap = coef[0, 0]
    tht = coef[0, 1]
    for e in range(1, n_par):
        kap = kap + coef[e, 0]
        tht = tht + coef[e, 1]
    lane = iota((n_par, width), 1)
    sub = iota((n_par, width), 0)
    first_row = lane < cg
    last_row = lane >= width - cg
    first_col = (sub == 0) & (lane % cg == 0)
    last_col = (sub == n_par - 1) & (lane % cg == cg - 1)
    up = pltpu.roll(tht, cg, 1)
    down = pltpu.roll(tht, width - cg, 1)
    left_of = jnp.concatenate([pltpu.roll(tht, 1, 1)[n_par - 1:], tht[:n_par - 1]], axis=0)
    right_of = jnp.concatenate([tht[1:], pltpu.roll(tht, width - 1, 1)[:1]], axis=0)
    north = 0.5 * (tht + jnp.where(first_row, tht, up))
    south = 0.5 * (tht + jnp.where(last_row, tht, down))
    west = 0.5 * (tht + jnp.where(first_col, tht, left_of))
    east = 0.5 * (tht + jnp.where(last_col, tht, right_of))
    diagonal = kap + north + south + west + east
    north = jnp.where(first_row, 0.0, north)
    south = jnp.where(last_row, 0.0, south)
    west = jnp.where(first_col, 0.0, west)
    east = jnp.where(last_col, 0.0, east)
    for index, value in enumerate((diagonal, north, south, west, east)):
        sf[index * n_par:(index + 1) * n_par, :] = value

    for copy in a_copies:
        copy.wait_recv()
    alphas, betas = chebyshev_scalars()
    tile = 16

    def row(index, block):
        return jnp.broadcast_to(sf[index * n_par + block:index * n_par + block + 1, :], (tile, width))

    def smooth(chunk, carry):
        start = pl.multiple_of(chunk * tile, tile)
        res = [gin[q, pl.ds(start, tile), :].astype(F32) for q in range(n_par)]
        dirn = res
        x = [alphas[0] * v for v in res]
        for sweep in range(1, SWEEPS):
            wrap_left = pltpu.roll(dirn[n_par - 1], 1, 1)
            wrap_right = pltpu.roll(dirn[0], width - 1, 1)
            fresh = []
            for q in range(n_par):
                u = dirn[q]
                w = dirn[q - 1] if q else wrap_left
                e = dirn[q + 1] if q + 1 < n_par else wrap_right
                value = (
                    row(0, q) * u
                    - row(1, q) * pltpu.roll(u, cg, 1)
                    - row(2, q) * pltpu.roll(u, width - cg, 1)
                    - row(3, q) * w
                    - row(4, q) * e
                )
                fresh.append(res[q] - alphas[sweep - 1] * value)
            res = fresh
            dirn = [r + betas[sweep] * v for r, v in zip(res, dirn)]
            x = [v + alphas[sweep] * u for v, u in zip(x, dirn)]
        place = iota((tile, width), 1) // cg
        for i in range(n_par):
            value = jnp.zeros((tile, width), F32)
            for q in range(n_par):
                shift = ((q - i) % n_par) * cg
                moved = pltpu.roll(x[q], shift, 1) if shift else x[q]
                value = jnp.where(place == q, moved, value)
            ysend[i, pl.ds(start, tile), :] = value.astype(BF16)
        return carry

    lax.fori_loop(0, fields // tile, smooth, 0)

    y_copies = []
    for e in range(1, n_par):
        target = (b + e) % n_par
        y_copies.append(push(ysend.at[target], sin.at[b], y_send.at[e], y_recv.at[e], {"par": target}))
    sin[b] = ysend[b]
    source = iota((width, width), 0)
    perm = ((source % cg) * n_par + source // cg == iota((width, width), 1)).astype(F32).astype(BF16)
    for copy in y_copies:
        copy.wait_recv()
    for q in range(n_par):
        sf[q * fields:(q + 1) * fields, :] = jnp.dot(sin[q], perm, preferred_element_type=F32)
    for r in range(here):
        freq_rows = sf[pl.ds(r, n_par * fields // here, stride=here), :].astype(BF16)
        out[r] = jnp.dot(wi[...], freq_rows, preferred_element_type=F32).astype(BF16)
    for copy in sends:
        copy.wait_send()


def table(freqs, negative_sine, scale):
    times = jnp.arange(NT, dtype=jnp.int32)
    phase = times[:, None] * freqs[None, :] % NT
    angle = phase.astype(F32) * (2.0 * math.pi / NT)
    return (jnp.where(negative_sine[None, :], -jnp.sin(angle), jnp.cos(angle)) / math.sqrt(scale)).astype(BF16)


def local(n_sens, n_par, data, green, freqs, sensor_order, kappa, theta):
    probes, sensors, _ = data.shape
    nfreq, _, _, cells = green.shape
    width = kappa.shape[1]
    kper = nfreq // n_par
    here = probes // n_sens
    lanes = here * 2 * kper
    fields = kper * 2 * here
    spad = round_up(sensors, 16)
    mine = lax.dynamic_slice_in_dim(freqs, lax.axis_index("par") * kper, kper)
    wide = round_up(lanes, 128)
    wf = table(jnp.tile(mine, wide // kper), jnp.arange(wide) // kper % 2 == 1, NT)
    wi = table(jnp.repeat(freqs, 2), jnp.arange(2 * nfreq) % 2 == 1, nfreq)
    chunks = 3
    flat = jnp.transpose(data, (1, 0, 2)).reshape(chunks, sensors * probes // chunks, NT)
    blocks = green.reshape(n_par, kper * sensors * 2, cells)
    order = jnp.pad(sensor_order, (0, spad - sensors), constant_values=-1).reshape(spad, 1)
    vmem = pl.BlockSpec(memory_space=pltpu.VMEM)
    anywhere = pl.BlockSpec(memory_space=pl.ANY)
    dma = pltpu.SemaphoreType.DMA
    nz = n_par // 2
    block = 2 * kper * here
    out = pl.pallas_call(
        functools.partial(kernel, n_sens, n_par, probes, sensors, kper),
        out_shape=jax.ShapeDtypeStruct((here, NT, width), BF16),
        in_specs=[anywhere, anywhere] + [vmem] * 5,
        out_specs=vmem,
        scratch_shapes=[
            pltpu.VMEM(flat.shape, BF16),
            pltpu.VMEM(blocks.shape, BF16),
            pltpu.VMEM(blocks.shape[1:], F32),
            pltpu.VMEM((nfreq, spad, 2 * cells), BF16),
            pltpu.VMEM((sensors * n_sens, wide), F32),
            pltpu.VMEM((n_sens, spad, n_sens * lanes), BF16),
            pltpu.VMEM((nz, 2, spad, n_sens * lanes), BF16),
            pltpu.VMEM((round_up(spad, 128) // 128, n_sens * lanes, 128), F32),
            pltpu.VMEM((n_par, n_sens, block, cells), BF16),
            pltpu.VMEM((n_par, n_sens - 1, block, cells), BF16),
            pltpu.VMEM((n_par, block, cells), BF16),
            pltpu.VMEM((n_par, block, cells), BF16),
            pltpu.VMEM((n_par, 2, n_par, width), F32),
            pltpu.VMEM((n_par, block, width), BF16),
            pltpu.VMEM((n_par, block, width), BF16),
            pltpu.VMEM((n_par * block, width), F32),
            dma((chunks + 1,)),
            dma((n_sens,)), dma((n_sens,)),
            dma((nz,)), dma((nz,)),
            dma((nz,)), dma((nz,)),
            dma((n_par, n_sens - 1)), dma((n_par, n_sens - 1)),
            dma((n_par,)), dma((n_par,)),
            dma((n_par,)), dma((n_par,)),
            dma((n_par,)), dma((n_par,)),
        ],
        compiler_params=pltpu.CompilerParams(
            collective_id=0, has_side_effects=True, vmem_limit_bytes=56 * 1024 * 1024
        ),
    )(flat, blocks, wf, wi, order, kappa, theta)
    return out.reshape(here, NT, 1, width)


def solution(mesh):
    placed = (
        P(None, "sens", None),
        P(None, "sens", None, "par"),
        P(),
        P("sens"),
        P("par", None),
        P("par", None),
    )
    return jax.shard_map(
        functools.partial(local, mesh.shape["sens"], mesh.shape["par"]),
        mesh=mesh, in_specs=placed, out_specs=P("sens", None, "par", None), check_vma=False,
    )
```

time: 260 us -> 72.1 us (0.28)
  local copies, waits for them, and re-layouts: 74.9 us -> 5.3 us
  blocking collectives: 66.4 us -> 0 us
  waiting for transfers between devices: 65.8 us -> 0 us
  Pallas kernels: 0 us -> 64 us
  other arithmetic: 18.4 us -> 2.54 us
  matrix products: 14.2 us -> 0 us
  between operations: 13.5 us -> 0.02 us
  starting transfers between devices: 5.73 us -> 0 us
    pallas_call x0 -> x1, Pallas kernels: none -> 64 us  [local(): pl.pallas_call(functools.partial(kernel, n_sens, n_par, probes, sensors,...]
    all_gather x2 -> x0, blocking collectives: 47.7 us -> none  [the longest x1 28 us: local(): lax.all_gather(theta, 'par', axis=0, tiled=True)]
    psum x1 -> x0, waiting for transfers between devices: 36.3 us -> none  [local(): lax.psum(partial_sum.astype(jnp.bfloat16), 'sens').astype(jnp.float32)]
    all_gather x1 -> x0, waiting for transfers between devices: 29.5 us -> none  [local(): spectra_all = lax.all_gather(spectra_local, 'sens', axis=1, tiled=True)]
    all_to_all x1 -> x0, blocking collectives: 18.7 us -> none  [local(): lax.all_to_all(solution, 'par', split_axis=1, concat_axis=0, tiled=True)]
    unnamed x8 -> x0, local copies, waits for them, and re-layouts: 17.6 us -> none
    convert_element_type x4 -> x0, local copies, waits for them, and re-layouts: 15.1 us -> none  [the longest x1 7.42 us: local(): moved = lax.all_to_all(field.reshape(groups, rows_all, col_groups, 1).ast...]
    reshape x2, local copies, waits for them, and re-layouts: 17.5 us -> 2.93 us  [the longest x1 2.18 us: local(): return out.reshape(here, NT, 1, width)]
  transfers between devices with their start and end apart: 3 -> 0, of which waited for: 2 -> 0; matrix products, arithmetic and copies ran while one was open for 5% -> 0% of each run, Pallas kernels for 0% -> 0%
where the time goes in v1:
time: 72.1 us; the launch traced here: 71.9 us
  Pallas kernels  64 us (89%)
  local copies, waits for them, and re-layouts  5.3 us (7%)
  other arithmetic  2.54 us (4%)
    pallas_call x1, Pallas kernels, local(): pl.pallas_call(functools.partial(kernel, n_sens, n_par, probes, sensors,...  64 us
    convert_element_type x1, other arithmetic, table(): (jnp.where(negative_sine[None, :], -jnp.sin(angle), jnp.cos(angle)) / mat...  2.52 us
    reshape x1, local copies, waits for them, and re-layouts, local(): return out.reshape(here, NT, 1, width)  2.18 us

profile of v1, /device:TPU:0, one launch (start us, length us, event | category | flops | bytes accessed | tf_op | source)
XLA Modules:
  0.0 71.9 jit_solution(18439545103071034931)
XLA Ops:
  0.0 0.7 %dynamic_slice.3 = s32[8]{0:T(128)S(1)} dynamic-slice(s32[64]{0:T(128)} %param.8, s32[]{:T(128)S(6)} %select_n.50), dynamic_slice_sizes={8} | dynamic-slice | bytes 68 | tf_op jit(solution)/shard_map/dynamic_slice | solution.py:325
  0.7 0.7 pad.4
  1.4 0.1 mul.41
  1.5 0.7 %broadcast_in_dim.22 = s32[64,2]{1,0:T(8,128)S(1)} broadcast(s32[64]{0:T(128)} %param.8), dimensions={0} | broadcast | bytes 768 | tf_op jit(solution)/shard_map/broadcast_in_dim | solution.py:328
  2.2 0.1 mul.46
  2.4 0.8 %copy.8.order = s32[160,1]{1,0:T(8,128)} copy(s32[160,1]{0,1:T(1,128)S(1)} %bitcast.9) | data formatting | bytes 1280 | tf_op jit(solution)/shard_map/reshape | solution.py:332
  3.1 2.5 %multiply_convert_fusion = (bf16[420,128]{1,0:T(8,128)(2,1)}, bf16[420,128]{1,0:T(8,128)(2,1)}) fusion(s32[128]{0:T(128)S(1)} %mul.46, pred[128]{0:T(512)(128)(4,1)S(1)} %fusion.11, s32[128]{0:T(128)S(1)} %mul.41, pred[128]{0:T(512)(128)(4,1)S(1)} %fusion.10), kind=kLoop, calls=%fused_computation.6 | loop fusion | flops 1397760 | bytes 216320 | tf_op jit(solution)/shard_map/convert_element_type | solution.py:313
  5.7 64.0 %shard_map.64 = bf16[8,420,128]{2,1,0:T(8,128)(2,1)} custom-call(bf16[3,1600,420]{2,1,0:T(8,128)(2,1)} %bitcast.6, bf16[8,2400,128]{2,1,0:T(8,128)(2,1)} %bitcast.7, bf16[420,128]{1,0:T(8,128)(2,1)} %get-tuple-element.6.wf, bf16[420,128]{1,0:T(8,128)(2,1)} %get-tuple-element.5.wi, s32[160,1]{1,0:T(8,128)} %copy.8.order, f32[1,128]{1,0:T(1,128)} %kappa.1, ...), custom_call_target="tpu_custom_call" | custom-call | tf_op jit(solution)/shard_map/pallas_call | solution.py:338
  69.7 2.2 %copy.9 = bf16[8,420,1,128]{3,0,2,1:T(8,128)(2,1)} copy(bf16[8,420,1,128]{3,1,0,2:T(8,128)(2,1)} %bitcast.8) | data formatting | bytes 1720320 | tf_op jit(solution)/shard_map/reshape | solution.py:373
  (3 shorter events, 0.0 us)

commit v2 on v1

--- a/solution.py
+++ b/solution.py
@@ -8,7 +8,6 @@
 from jax.experimental.pallas import tpu as pltpu
 from jax.sharding import PartitionSpec as P
 
-NT = 420
 SWEEPS = 6
 lower_bound = 0.05
 upper_bound = 16.5
@@ -46,11 +45,35 @@
     return -(-value // unit) * unit
 
 
+def ring_place(z, size):
+    odd = z % 2
+    return odd * ((z + 1) // 2) + (1 - odd) * ((size - z // 2) % size)
+
+
+def ring_member(place, size):
+    back = ((place + size - 1) % size) // max(size // 2, 1)
+    return (1 - back) * (2 * place - 1) + back * (2 * ((size - place) % size))
+
+
+def table(freqs, chosen, quarter, nt, scale):
+    lanes_freq = jnp.dot(freqs, chosen, preferred_element_type=F32)[:1]
+    shape = (nt, chosen.shape[1])
+    turn = iota(shape, 0).astype(F32) * lanes_freq + quarter.astype(F32) * (nt // 4)
+    turn = turn - nt * jnp.floor((turn + 0.5) * (1.0 / nt))
+    arc = (nt // 4 - jnp.abs(turn - nt // 2)) * (2.0 * math.pi / nt)
+    square = arc * arc
+    sine = jnp.full(shape, 1.0 / math.factorial(13), F32)
+    for power in (11, 9, 7, 5, 3, 1):
+        sign = -1.0 if power % 4 == 3 else 1.0
+        sine = sine * square + sign / math.factorial(power)
+    return (sine * arc * (-1.0 / math.sqrt(scale))).astype(BF16)
+
+
 def kernel(
     n_sens, n_par, probes, sensors, kper,
-    data_hbm, green_hbm, wf, wi, order, kappa, theta,
+    data_hbm, green_hbm, freqs, order, kappa, theta,
     out,
-    data_v, green_v, green_f, green_s, spec_f, ubuf, vbuf, vt, part, rsbuf, adj, gin,
+    wf, wi, tall, data_v, green_v, green_f, green_s, spec_f, ubuf, vbuf, vt, part, rsbuf, adj, gin,
     coef, ysend, sin, sf,
     load_sem, u_send, u_recv, z_send, z_recv, x_send, x_recv, rs_send, rs_recv,
     a_send, a_recv, c_send, c_recv, y_send, y_recv,
@@ -58,12 +81,12 @@
     a = lax.axis_index("sens")
     b = lax.axis_index("par")
     nz = n_par // 2
-    zpos = b // 2
     xpos = b % 2
+    zring = ring_place(b // 2, nz)
     here = probes // n_sens
     lanes = here * 2 * kper
     fields = kper * 2 * here
-    spad = ubuf.shape[1]
+    spad = ubuf.shape[2]
     groups = n_sens
     width = out.shape[-1]
     cg = width // n_par
@@ -89,6 +112,13 @@
     green_load = pltpu.make_async_copy(green_hbm, green_v, load_sem.at[chunks])
     green_load.start()
 
+    nt = wi.shape[0]
+    nfreq = freqs.shape[1]
+    freq_rows = jnp.broadcast_to(freqs[...], (8, nfreq)).astype(F32).astype(BF16)
+    wide = wf.shape[1]
+    chosen = iota((nfreq, wide), 0) == b * kper + iota((nfreq, wide), 1) % kper
+    wf[...] = table(freq_rows, chosen.astype(F32).astype(BF16), iota((nt, wide), 1) // kper % 2, nt, nt)
+
     pick = (iota((width, width), 0) // n_par + b * cg == iota((width, width), 1)).astype(F32)
     own = iota((n_par, width), 1) % n_par == iota((n_par, width), 0)
     for index, ref in enumerate((kappa, theta)):
@@ -96,16 +126,15 @@
         coef[0, index] = jnp.dot(spread, pick, precision=lax.Precision.HIGHEST, preferred_element_type=F32)
 
     rows = data_v.shape[1]
-    wide = wf.shape[1]
     keep = iota((rows // here, here, wide), 2) // (2 * kper) == iota((rows // here, here, wide), 1)
     for c in range(chunks):
         loads[c].wait()
         prod = jnp.dot(data_v[c], wf[...], preferred_element_type=F32)
         prod = jnp.where(keep, prod.reshape(rows // here, here, wide), 0.0)
         spec_f[c * (rows // here):(c + 1) * (rows // here), :] = jnp.sum(prod, axis=1)
-    ubuf[0, spad - 16:, :] = jnp.zeros((16, groups * lanes), BF16)
+    ubuf[0, 0, spad - 16:, :] = jnp.zeros((16, groups * lanes), BF16)
     for g in range(groups):
-        ubuf[0, :sensors, g * lanes:(g + 1) * lanes] = spec_f[pl.ds(g, sensors, stride=groups), :][:, :lanes].astype(BF16)
+        ubuf[0, 0, :sensors, g * lanes:(g + 1) * lanes] = spec_f[pl.ds(g, sensors, stride=groups), :][:, :lanes].astype(BF16)
 
     pl.semaphore_wait(barrier, n_sens + n_par - 2)
     sends = []
@@ -118,7 +147,21 @@
         sends.append(copy)
         return copy
 
-    u_copies = [push(ubuf.at[0], ubuf.at[e], u_send.at[e], u_recv.at[e], sens_peer(e)) for e in range(1, n_sens)]
+    ny = n_sens // 2
+    cpos = a % 2
+    yring = ring_place(a // 2, ny)
+    core_peer = {"sens": (a // 2) * 2 + (1 - cpos)}
+    y_next = {"sens": ring_member((yring + 1) % ny, ny) * 2 + cpos}
+    u_copies = {}
+
+    def gather_u(d):
+        if d:
+            u_copies[d, 0].wait_recv()
+        if d + 1 < ny:
+            u_copies[d + 1, 0] = push(ubuf.at[d, 0], ubuf.at[d + 1, 0], u_send.at[d, 0], u_recv.at[d + 1, 0], y_next)
+        u_copies[d, 1] = push(ubuf.at[d, 0], ubuf.at[d, 1], u_send.at[d, 1], u_recv.at[d, 1], core_peer)
+
+    gather_u(0)
     c_copies = [push(coef.at[0], coef.at[e], c_send.at[e], c_recv.at[e], par_peer(e)) for e in range(1, n_par)]
 
     green_load.wait()
@@ -134,41 +177,67 @@
 
     lax.fori_loop(0, n_par, split, 0)
 
-    picked = jnp.zeros((spad, groups * lanes), F32)
-    wanted = jnp.broadcast_to(order[...], (spad, spad))
-    for e in range(n_sens):
-        if e:
-            u_copies[e - 1].wait_recv()
-        base = ((a - e + n_sens) % n_sens) * sensors
-        position = iota((spad, spad), 1)
-        match = ((wanted == position + base) & (position < sensors)).astype(F32).astype(BF16)
-        picked = picked + jnp.dot(match, ubuf[e], preferred_element_type=F32)
-    vbuf[0, 0] = picked.astype(BF16)
-
-    partner = {"par": zpos * 2 + (1 - xpos)}
+    column = jnp.transpose(jnp.broadcast_to(order[...].astype(F32), (128, sensors)))[:, :1]
+    wanted = jnp.broadcast_to(column, (sensors, spad))
+    picked = jnp.zeros((sensors, groups * lanes), F32)
+    position = iota((sensors, spad), 1)
+    for d in range(ny):
+        if d:
+            gather_u(d)
+        for ci in range(2):
+            if ci:
+                u_copies[d, 1].wait_recv()
+            source = ring_member((yring - d + ny) % ny, ny) * 2 + (cpos if ci == 0 else 1 - cpos)
+            match = (wanted == (position + source * sensors).astype(F32)) & (position < sensors)
+            picked = picked + jnp.dot(match.astype(F32).astype(BF16), ubuf[d, ci], preferred_element_type=F32)
+    vbuf[0, 0, spad - 16:, :] = jnp.zeros((16, groups * lanes), BF16)
+    vbuf[0, 0, :sensors, :] = picked.astype(BF16)
+
+    partner = {"par": (b // 2) * 2 + (1 - xpos)}
+    z_next = {"par": ring_member((zring + 1) % nz, nz) * 2 + xpos}
+    cut = round_up(spad // 2, 16) if nz > 2 else spad
     z_copies = {}
     x_copies = {}
-    for d in range(1, nz):
-        peer = {"par": ((zpos + d) % nz) * 2 + xpos}
-        z_copies[d] = push(vbuf.at[0, 0], vbuf.at[d, 0], z_send.at[d], z_recv.at[d], peer)
-    x_copies[0] = push(vbuf.at[0, 0], vbuf.at[0, 1], x_send.at[0], x_recv.at[0], partner)
+
+    def gather_v(d):
+        if d:
+            z_copies[d].wait_recv()
+        if d + 1 < nz:
+            z_copies[d + 1] = push(vbuf.at[d, 0], vbuf.at[d + 1, 0], z_send.at[d], z_recv.at[d + 1], z_next)
+        size = cut if d + 1 == nz else spad
+        x_copies[d] = push(
+            vbuf.at[d, 0, pl.ds(0, size)], vbuf.at[d, 1, pl.ds(0, size)], x_send.at[d], x_recv.at[d], partner
+        )
+
+    gather_v(0)
+    freq_pair = iota((nfreq, 2 * nfreq), 0) == iota((nfreq, 2 * nfreq), 1) // 2
+    wi[...] = table(freq_rows, freq_pair.astype(F32).astype(BF16), iota((nt, 2 * nfreq), 1) % 2, nt, nfreq)
 
     rs_copies = {}
     a_copies = []
-    steps = [(d, xi) for d in range(nz) for xi in range(2)]
+    steps = [(0, 0)]
+    for d in range(1, nz):
+        steps += [(d, 0), (d - 1, 1)]
+    steps.append((nz - 1, 1))
 
     def owner(step):
         d, xi = step
         other = xpos if xi == 0 else 1 - xpos
-        return ((zpos - d + nz) % nz) * 2 + other
+        return ring_member((zring - d + nz) % nz, nz) * 2 + other
 
     def products(index):
         d, xi = steps[index]
         if xi:
             x_copies[d].wait_recv()
+            if d + 2 == nz and cut < spad:
+                rest = pl.ds(cut, spad - cut)
+                z_copies[nz] = push(
+                    vbuf.at[d, 1, rest], vbuf.at[d + 1, 1, rest], z_send.at[nz], z_recv.at[nz], z_next
+                )
+            if d + 1 == nz and cut < spad:
+                z_copies[nz].wait_recv()
         elif d:
-            z_copies[d].wait_recv()
-            x_copies[d] = push(vbuf.at[d, 0], vbuf.at[d, 1], x_send.at[d], x_recv.at[d], partner)
+            gather_v(d)
         block = owner(steps[index])
         for t in range(vt.shape[0]):
             size = min(spad - t * 128, 128)
@@ -211,8 +280,9 @@
 
     for index in range(n_par):
         products(index)
-        if index:
-            reduce(index - 1)
+        if index >= 2:
+            reduce(index - 2)
+    reduce(n_par - 2)
     reduce(n_par - 1)
 
     for copy in c_copies:
@@ -248,50 +318,65 @@
         copy.wait_recv()
     alphas, betas = chebyshev_scalars()
     tile = 16
+    low = 8
 
     def row(index, block):
-        return jnp.broadcast_to(sf[index * n_par + block:index * n_par + block + 1, :], (tile, width))
+        return jnp.broadcast_to(sf[index * n_par + block:index * n_par + block + 1, :], (low, width))
 
     def smooth(chunk, carry):
         start = pl.multiple_of(chunk * tile, tile)
-        res = [gin[q, pl.ds(start, tile), :].astype(F32) for q in range(n_par)]
-        dirn = res
-        x = [alphas[0] * v for v in res]
-        for sweep in range(1, SWEEPS):
-            wrap_left = pltpu.roll(dirn[n_par - 1], 1, 1)
-            wrap_right = pltpu.roll(dirn[0], width - 1, 1)
-            fresh = []
-            for q in range(n_par):
-                u = dirn[q]
-                w = dirn[q - 1] if q else wrap_left
-                e = dirn[q + 1] if q + 1 < n_par else wrap_right
-                value = (
-                    row(0, q) * u
-                    - row(1, q) * pltpu.roll(u, cg, 1)
-                    - row(2, q) * pltpu.roll(u, width - cg, 1)
-                    - row(3, q) * w
-                    - row(4, q) * e
+        loaded = [gin[q, pl.ds(start, tile), :].astype(F32) for q in range(n_par)]
+        place = iota((low, width), 1) // cg
+        rows_out = []
+        for part_index in range(tile // low):
+            res = [v[part_index * low:(part_index + 1) * low] for v in loaded]
+            dirn = res
+            x = [alphas[0] * v for v in res]
+            for sweep in range(1, SWEEPS):
+                wrap_left = pltpu.roll(dirn[n_par - 1], 1, 1)
+                wrap_right = pltpu.roll(dirn[0], width - 1, 1)
+                fresh = []
+                for q in range(n_par):
+                    u = dirn[q]
+                    w = dirn[q - 1] if q else wrap_left
+                    e = dirn[q + 1] if q + 1 < n_par else wrap_right
+                    value = (
+                        row(0, q) * u
+                        - row(1, q) * pltpu.roll(u, cg, 1)
+                        - row(2, q) * pltpu.roll(u, width - cg, 1)
+                        - row(3, q) * w
+                        - row(4, q) * e
+                    )
+                    fresh.append(res[q] - alphas[sweep - 1] * value)
+                res = fresh
+                dirn = [r + betas[sweep] * v for r, v in zip(res, dirn)]
+                x = [v + alphas[sweep] * u for v, u in zip(x, dirn)]
+            moved_rows = []
+            for i in range(n_par):
+                value = x[i]
+                for q in range(n_par):
+                    if q != i:
+                        value = jnp.where(place == q, pltpu.roll(x[q], ((q - i) % n_par) * cg, 1), value)
+                moved_rows.append(value)
+            rows_out.append(moved_rows)
+        for i in range(n_par):
+            both = jnp.concatenate([piece[i] for piece in rows_out], axis=0)
+            ysend[i, pl.ds(start, tile), :] = both.astype(BF16)
+        return carry
+
+    cuts = [0, fields // tile // 2, fields // tile]
+    y_copies = []
+    for half in range(2):
+        lax.fori_loop(cuts[half], cuts[half + 1], smooth, 0)
+        span = pl.ds(cuts[half] * tile, (cuts[half + 1] - cuts[half]) * tile)
+        for e in range(1, n_par):
+            target = (b + e) % n_par
+            y_copies.append(
+                push(
+                    ysend.at[target, span], sin.at[b, span],
+                    y_send.at[half, e], y_recv.at[half, e], {"par": target},
                 )
-                fresh.append(res[q] - alphas[sweep - 1] * value)
-            res = fresh
-            dirn = [r + betas[sweep] * v for r, v in zip(res, dirn)]
-            x = [v + alphas[sweep] * u for v, u in zip(x, dirn)]
-        place = iota((tile, width), 1) // cg
-        for i in range(n_par):
-            value = jnp.zeros((tile, width), F32)
-            for q in range(n_par):
-                shift = ((q - i) % n_par) * cg
-                moved = pltpu.roll(x[q], shift, 1) if shift else x[q]
-                value = jnp.where(place == q, moved, value)
-            ysend[i, pl.ds(start, tile), :] = value.astype(BF16)
-        return carry
-
-    lax.fori_loop(0, fields // tile, smooth, 0)
-
-    y_copies = []
-    for e in range(1, n_par):
-        target = (b + e) % n_par
-        y_copies.append(push(ysend.at[target], sin.at[b], y_send.at[e], y_recv.at[e], {"par": target}))
+            )
     sin[b] = ysend[b]
     source = iota((width, width), 0)
     perm = ((source % cg) * n_par + source // cg == iota((width, width), 1)).astype(F32).astype(BF16)
@@ -300,21 +385,15 @@
     for q in range(n_par):
         sf[q * fields:(q + 1) * fields, :] = jnp.dot(sin[q], perm, preferred_element_type=F32)
     for r in range(here):
-        freq_rows = sf[pl.ds(r, n_par * fields // here, stride=here), :].astype(BF16)
-        out[r] = jnp.dot(wi[...], freq_rows, preferred_element_type=F32).astype(BF16)
+        mine = sf[pl.ds(r, n_par * fields // here, stride=here), :].astype(BF16)
+        tall[pl.ds(r, nt, stride=here), :] = jnp.dot(wi[...], mine, preferred_element_type=F32)
+    out[...] = tall[...].astype(BF16)
     for copy in sends:
         copy.wait_send()
 
 
-def table(freqs, negative_sine, scale):
-    times = jnp.arange(NT, dtype=jnp.int32)
-    phase = times[:, None] * freqs[None, :] % NT
-    angle = phase.astype(F32) * (2.0 * math.pi / NT)
-    return (jnp.where(negative_sine[None, :], -jnp.sin(angle), jnp.cos(angle)) / math.sqrt(scale)).astype(BF16)
-
-
 def local(n_sens, n_par, data, green, freqs, sensor_order, kappa, theta):
-    probes, sensors, _ = data.shape
+    probes, sensors, nt = data.shape
     nfreq, _, _, cells = green.shape
     width = kappa.shape[1]
     kper = nfreq // n_par
@@ -322,14 +401,10 @@
     lanes = here * 2 * kper
     fields = kper * 2 * here
     spad = round_up(sensors, 16)
-    mine = lax.dynamic_slice_in_dim(freqs, lax.axis_index("par") * kper, kper)
     wide = round_up(lanes, 128)
-    wf = table(jnp.tile(mine, wide // kper), jnp.arange(wide) // kper % 2 == 1, NT)
-    wi = table(jnp.repeat(freqs, 2), jnp.arange(2 * nfreq) % 2 == 1, nfreq)
     chunks = 3
-    flat = jnp.transpose(data, (1, 0, 2)).reshape(chunks, sensors * probes // chunks, NT)
+    flat = jnp.transpose(data, (1, 0, 2)).reshape(chunks, sensors * probes // chunks, nt)
     blocks = green.reshape(n_par, kper * sensors * 2, cells)
-    order = jnp.pad(sensor_order, (0, spad - sensors), constant_values=-1).reshape(spad, 1)
     vmem = pl.BlockSpec(memory_space=pltpu.VMEM)
     anywhere = pl.BlockSpec(memory_space=pl.ANY)
     dma = pltpu.SemaphoreType.DMA
@@ -337,16 +412,19 @@
     block = 2 * kper * here
     out = pl.pallas_call(
         functools.partial(kernel, n_sens, n_par, probes, sensors, kper),
-        out_shape=jax.ShapeDtypeStruct((here, NT, width), BF16),
-        in_specs=[anywhere, anywhere] + [vmem] * 5,
+        out_shape=jax.ShapeDtypeStruct((nt * here, width), BF16),
+        in_specs=[anywhere, anywhere] + [vmem] * 4,
         out_specs=vmem,
         scratch_shapes=[
+            pltpu.VMEM((nt, wide), BF16),
+            pltpu.VMEM((nt, 2 * nfreq), BF16),
+            pltpu.VMEM((nt * here, width), F32),
             pltpu.VMEM(flat.shape, BF16),
             pltpu.VMEM(blocks.shape, BF16),
             pltpu.VMEM(blocks.shape[1:], F32),
             pltpu.VMEM((nfreq, spad, 2 * cells), BF16),
             pltpu.VMEM((sensors * n_sens, wide), F32),
-            pltpu.VMEM((n_sens, spad, n_sens * lanes), BF16),
+            pltpu.VMEM((n_sens // 2, 2, spad, n_sens * lanes), BF16),
             pltpu.VMEM((nz, 2, spad, n_sens * lanes), BF16),
             pltpu.VMEM((round_up(spad, 128) // 128, n_sens * lanes, 128), F32),
             pltpu.VMEM((n_par, n_sens, block, cells), BF16),
@@ -358,19 +436,19 @@
             pltpu.VMEM((n_par, block, width), BF16),
             pltpu.VMEM((n_par * block, width), F32),
             dma((chunks + 1,)),
-            dma((n_sens,)), dma((n_sens,)),
-            dma((nz,)), dma((nz,)),
+            dma((n_sens // 2, 2)), dma((n_sens // 2, 2)),
+            dma((nz + 1,)), dma((nz + 1,)),
             dma((nz,)), dma((nz,)),
             dma((n_par, n_sens - 1)), dma((n_par, n_sens - 1)),
             dma((n_par,)), dma((n_par,)),
             dma((n_par,)), dma((n_par,)),
-            dma((n_par,)), dma((n_par,)),
+            dma((2, n_par)), dma((2, n_par)),
         ],
         compiler_params=pltpu.CompilerParams(
             collective_id=0, has_side_effects=True, vmem_limit_bytes=56 * 1024 * 1024
         ),
-    )(flat, blocks, wf, wi, order, kappa, theta)
-    return out.reshape(here, NT, 1, width)
+    )(flat, blocks, freqs.reshape(1, nfreq), sensor_order.reshape(1, sensors), kappa, theta)
+    return jnp.transpose(out.reshape(nt, here, 1, width), (1, 0, 2, 3))
 
 
 def solution(mesh):

time: 72.1 us -> 58.4 us (0.81)
  Pallas kernels: 64 us -> 56.1 us
  local copies, waits for them, and re-layouts: 5.3 us -> 2.12 us
  other arithmetic: 2.54 us -> 0 us
    pallas_call x1, Pallas kernels: 64 us -> 56.1 us  [local(): pl.pallas_call(functools.partial(kernel, n_sens, n_par, probes, sensors,...]
    reshape x2 -> x0, local copies, waits for them, and re-layouts: 2.93 us -> none  [the longest x1 2.18 us: local(): return out.reshape(here, NT, 1, width)]
    convert_element_type x1 -> x0, other arithmetic: 2.52 us -> none  [table(): (jnp.where(negative_sine[None, :], -jnp.sin(angle), jnp.cos(angle)) / mat...]
    unnamed x0 -> x1, local copies, waits for them, and re-layouts: none -> 2.12 us
    broadcast_in_dim x1 -> x0, local copies, waits for them, and re-layouts: 0.73 us -> none  [local(): wi = table(jnp.repeat(freqs, 2), jnp.arange(2 * nfreq) % 2 == 1, nfreq)]
    dynamic_slice x1 -> x0, local copies, waits for them, and re-layouts: 0.73 us -> none  [local(): mine = lax.dynamic_slice_in_dim(freqs, lax.axis_index('par') * kper, kper)]
where the time goes in v2:
time: 58.4 us; the launch traced here: 58.3 us
  Pallas kernels  56.1 us (96%)
  local copies, waits for them, and re-layouts  2.12 us (4%)
    pallas_call x1, Pallas kernels, local(): pl.pallas_call(functools.partial(kernel, n_sens, n_par, probes, sensors,...  56.1 us
    unnamed x1, local copies, waits for them, and re-layouts  2.12 us

profile of v2, /device:TPU:0, one launch (start us, length us, event | category | flops | bytes accessed | tf_op | source)
XLA Modules:
  0.0 58.3 jit_solution(10265417276835752524)
XLA Ops:
  0.0 56.1 %shard_map.64 = bf16[3360,128]{1,0:T(8,128)(2,1)} custom-call(bf16[3,1600,420]{2,1,0:T(8,128)(2,1)} %bitcast.11, bf16[8,2400,128]{2,1,0:T(8,128)(2,1)} %bitcast.12, s32[1,64]{1,0:T(1,128)} %bitcast.15, s32[1,150]{1,0:T(1,128)} %bitcast.14, f32[1,128]{1,0:T(1,128)} %kappa.1, f32[1,128]{1,0:T(1,128)} %theta.1), custom_call_target="tpu_custom_call" | custom-call | tf_op jit(solution)/shard_map/pallas_call | solution.py:413
  56.1 2.1 %copy.9 = bf16[8,420,1,128]{3,0,2,1:T(8,128)(2,1)} copy(bf16[8,420,1,128]{3,0,2,1:T(8,128)(2,1)} %bitcast.13) | data formatting | bytes 1720320

commit v3 on v2

--- a/solution.py
+++ b/solution.py
@@ -72,8 +72,8 @@
 def kernel(
     n_sens, n_par, probes, sensors, kper,
     data_hbm, green_hbm, freqs, order, kappa, theta,
-    out,
-    wf, wi, tall, data_v, green_v, green_f, green_s, spec_f, ubuf, vbuf, vt, part, rsbuf, adj, gin,
+    out, wi_out,
+    wf, data_v, green_v, green_f, green_s, spec_f, ubuf, vbuf, vt, part, rsbuf, adj, gin,
     coef, ysend, sin, sf,
     load_sem, u_send, u_recv, z_send, z_recv, x_send, x_recv, rs_send, rs_recv,
     a_send, a_recv, c_send, c_recv, y_send, y_recv,
@@ -112,12 +112,12 @@
     green_load = pltpu.make_async_copy(green_hbm, green_v, load_sem.at[chunks])
     green_load.start()
 
-    nt = wi.shape[0]
+    nt = wf.shape[0]
     nfreq = freqs.shape[1]
     freq_rows = jnp.broadcast_to(freqs[...], (8, nfreq)).astype(F32).astype(BF16)
     wide = wf.shape[1]
-    chosen = iota((nfreq, wide), 0) == b * kper + iota((nfreq, wide), 1) % kper
-    wf[...] = table(freq_rows, chosen.astype(F32).astype(BF16), iota((nt, wide), 1) // kper % 2, nt, nt)
+    chosen = iota((nfreq, wide), 0) == b * kper + iota((nfreq, wide), 1) // (2 * here)
+    wf[...] = table(freq_rows, chosen.astype(F32).astype(BF16), iota((nt, wide), 1) // here % 2, nt, nt)
 
     pick = (iota((width, width), 0) // n_par + b * cg == iota((width, width), 1)).astype(F32)
     own = iota((n_par, width), 1) % n_par == iota((n_par, width), 0)
@@ -126,15 +126,23 @@
         coef[0, index] = jnp.dot(spread, pick, precision=lax.Precision.HIGHEST, preferred_element_type=F32)
 
     rows = data_v.shape[1]
-    keep = iota((rows // here, here, wide), 2) // (2 * kper) == iota((rows // here, here, wide), 1)
+    sensors_chunk = sensors // chunks
+    stack = round_up(sensors_chunk, 8)
+    qshape = (groups * stack, rows)
+    add_rows = iota(qshape, 1) // here == iota(qshape, 0) % stack * groups + iota(qshape, 0) // stack
+    add_rows = add_rows.astype(F32).astype(BF16)
+    lane = iota((rows, wide), 1)
+    keep = (lane % here == iota((rows, wide), 0) % here) & (lane < lanes)
     for c in range(chunks):
         loads[c].wait()
         prod = jnp.dot(data_v[c], wf[...], preferred_element_type=F32)
-        prod = jnp.where(keep, prod.reshape(rows // here, here, wide), 0.0)
-        spec_f[c * (rows // here):(c + 1) * (rows // here), :] = jnp.sum(prod, axis=1)
+        prod = jnp.where(keep, prod, 0.0).astype(BF16)
+        sums = jnp.dot(add_rows, prod, preferred_element_type=F32)
+        for g in range(groups):
+            spec_f[g, c * sensors_chunk:(c + 1) * sensors_chunk, :] = sums[g * stack:g * stack + sensors_chunk]
     ubuf[0, 0, spad - 16:, :] = jnp.zeros((16, groups * lanes), BF16)
     for g in range(groups):
-        ubuf[0, 0, :sensors, g * lanes:(g + 1) * lanes] = spec_f[pl.ds(g, sensors, stride=groups), :][:, :lanes].astype(BF16)
+        ubuf[0, 0, :sensors, g * lanes:(g + 1) * lanes] = spec_f[g][:, :lanes].astype(BF16)
 
     pl.semaphore_wait(barrier, n_sens + n_par - 2)
     sends = []
@@ -175,15 +183,17 @@
                 green_s[block * kper + k, :sensors, c * width:(c + 1) * width] = piece.astype(BF16)
         return carry
 
-    lax.fori_loop(0, n_par, split, 0)
+    bounds = [n_par * d // ny for d in range(ny + 1)]
+    for d in range(ny):
+        if d:
+            gather_u(d)
+        lax.fori_loop(bounds[d], bounds[d + 1], split, 0)
 
     column = jnp.transpose(jnp.broadcast_to(order[...].astype(F32), (128, sensors)))[:, :1]
     wanted = jnp.broadcast_to(column, (sensors, spad))
     picked = jnp.zeros((sensors, groups * lanes), F32)
     position = iota((sensors, spad), 1)
     for d in range(ny):
-        if d:
-            gather_u(d)
         for ci in range(2):
             if ci:
                 u_copies[d, 1].wait_recv()
@@ -211,7 +221,10 @@
 
     gather_v(0)
     freq_pair = iota((nfreq, 2 * nfreq), 0) == iota((nfreq, 2 * nfreq), 1) // 2
-    wi[...] = table(freq_rows, freq_pair.astype(F32).astype(BF16), iota((nt, 2 * nfreq), 1) % 2, nt, nfreq)
+    wi = table(freq_rows, freq_pair.astype(F32).astype(BF16), iota((nt, 2 * nfreq), 1) % 2, nt, nfreq)
+    steps_here = wi_out.shape[1]
+    for p in range(wi_out.shape[0]):
+        wi_out[p] = wi[p * steps_here:(p + 1) * steps_here]
 
     rs_copies = {}
     a_copies = []
@@ -239,23 +252,19 @@
         elif d:
             gather_v(d)
         block = owner(steps[index])
-        for t in range(vt.shape[0]):
-            size = min(spad - t * 128, 128)
-            vt[t, :, :size] = jnp.transpose(vbuf[d, xi, t * 128:t * 128 + size, :].astype(F32))
-        half = probes
+        vt[...] = jnp.transpose(vbuf[d, xi])
+        pair = 2 * here
         for k in range(kper):
-            left = []
-            for t in range(vt.shape[0]):
-                real = vt[t, pl.ds(k, half, stride=2 * kper), :]
-                imag = vt[t, pl.ds(kper + k, half, stride=2 * kper), :]
-                left.append(jnp.concatenate([real, imag], axis=0).astype(BF16)[:, :min(spad - t * 128, 128)])
-            left = jnp.concatenate(left, axis=1)
+            left = jnp.concatenate(
+                [vt[g * lanes + k * pair:g * lanes + (k + 1) * pair, :] for g in range(groups)], axis=0
+            )
             prod = jnp.dot(left, green_s[block * kper + k], preferred_element_type=F32)
-            re = prod[:half, :width] + prod[half:, width:]
-            im = prod[half:, :width] - prod[:half, width:]
             for g in range(groups):
-                both = jnp.concatenate([re[g * here:(g + 1) * here], im[g * here:(g + 1) * here]], axis=0)
-                part[index, g, k * 2 * here:(k + 1) * 2 * here, :] = both.astype(BF16)
+                real = prod[g * pair:g * pair + here]
+                imag = prod[g * pair + here:(g + 1) * pair]
+                re = real[:, :width] + imag[:, width:]
+                im = imag[:, :width] - real[:, width:]
+                part[index, g, k * pair:(k + 1) * pair, :] = jnp.concatenate([re, im], axis=0).astype(BF16)
         rs_copies[index] = [
             push(
                 part.at[index, (a + e) % n_sens], rsbuf.at[index, e - 1],
@@ -378,18 +387,29 @@
                 )
             )
     sin[b] = ysend[b]
-    source = iota((width, width), 0)
-    perm = ((source % cg) * n_par + source // cg == iota((width, width), 1)).astype(F32).astype(BF16)
     for copy in y_copies:
         copy.wait_recv()
-    for q in range(n_par):
-        sf[q * fields:(q + 1) * fields, :] = jnp.dot(sin[q], perm, preferred_element_type=F32)
-    for r in range(here):
-        mine = sf[pl.ds(r, n_par * fields // here, stride=here), :].astype(BF16)
-        tall[pl.ds(r, nt, stride=here), :] = jnp.dot(wi[...], mine, preferred_element_type=F32)
-    out[...] = tall[...].astype(BF16)
+    out[...] = sin[...]
     for copy in sends:
         copy.wait_send()
+
+
+def inverse_kernel(n_par, here, smoothed, wi, out, sf, tall):
+    width = out.shape[1]
+    cg = width // n_par
+    fields = smoothed.shape[0]
+
+    @pl.when(pl.program_id(0) == 0)
+    def _():
+        source = iota((width, width), 0)
+        perm = ((source % cg) * n_par + source // cg == iota((width, width), 1)).astype(F32).astype(BF16)
+        sf[...] = jnp.dot(smoothed[...], perm, preferred_element_type=F32)
+
+    steps = tall.shape[0] // here
+    for r in range(here):
+        mine = sf[pl.ds(r, fields // here, stride=here), :].astype(BF16)
+        tall[pl.ds(r, steps, stride=here), :] = jnp.dot(wi[0], mine, preferred_element_type=F32)
+    out[...] = tall[...].astype(BF16)
 
 
 def local(n_sens, n_par, data, green, freqs, sensor_order, kappa, theta):
@@ -403,6 +423,7 @@
     spad = round_up(sensors, 16)
     wide = round_up(lanes, 128)
     chunks = 3
+    pieces = 3
     flat = jnp.transpose(data, (1, 0, 2)).reshape(chunks, sensors * probes // chunks, nt)
     blocks = green.reshape(n_par, kper * sensors * 2, cells)
     vmem = pl.BlockSpec(memory_space=pltpu.VMEM)
@@ -410,23 +431,24 @@
     dma = pltpu.SemaphoreType.DMA
     nz = n_par // 2
     block = 2 * kper * here
-    out = pl.pallas_call(
+    smoothed, wi = pl.pallas_call(
         functools.partial(kernel, n_sens, n_par, probes, sensors, kper),
-        out_shape=jax.ShapeDtypeStruct((nt * here, width), BF16),
+        out_shape=[
+            jax.ShapeDtypeStruct((n_par, fields, width), BF16),
+            jax.ShapeDtypeStruct((pieces, nt // pieces, 2 * nfreq), BF16),
+        ],
         in_specs=[anywhere, anywhere] + [vmem] * 4,
-        out_specs=vmem,
+        out_specs=[vmem, vmem],
         scratch_shapes=[
             pltpu.VMEM((nt, wide), BF16),
-            pltpu.VMEM((nt, 2 * nfreq), BF16),
-            pltpu.VMEM((nt * here, width), F32),
             pltpu.VMEM(flat.shape, BF16),
             pltpu.VMEM(blocks.shape, BF16),
             pltpu.VMEM(blocks.shape[1:], F32),
             pltpu.VMEM((nfreq, spad, 2 * cells), BF16),
-            pltpu.VMEM((sensors * n_sens, wide), F32),
+            pltpu.VMEM((n_sens, sensors, wide), F32),
             pltpu.VMEM((n_sens // 2, 2, spad, n_sens * lanes), BF16),
             pltpu.VMEM((nz, 2, spad, n_sens * lanes), BF16),
-            pltpu.VMEM((round_up(spad, 128) // 128, n_sens * lanes, 128), F32),
+            pltpu.VMEM((n_sens * lanes, spad), BF16),
             pltpu.VMEM((n_par, n_sens, block, cells), BF16),
             pltpu.VMEM((n_par, n_sens - 1, block, cells), BF16),
             pltpu.VMEM((n_par, block, cells), BF16),
@@ -448,6 +470,21 @@
             collective_id=0, has_side_effects=True, vmem_limit_bytes=56 * 1024 * 1024
         ),
     )(flat, blocks, freqs.reshape(1, nfreq), sensor_order.reshape(1, sensors), kappa, theta)
+    total = n_par * fields
+    out = pl.pallas_call(
+        functools.partial(inverse_kernel, n_par, here),
+        out_shape=jax.ShapeDtypeStruct((nt * here, width), BF16),
+        grid=(pieces,),
+        in_specs=[
+            pl.BlockSpec((total, width), lambda i: (0, 0)),
+            pl.BlockSpec((1, nt // pieces, 2 * nfreq), lambda i: (i, 0, 0)),
+        ],
+        out_specs=pl.BlockSpec((nt * here // pieces, width), lambda i: (i, 0)),
+        scratch_shapes=[
+            pltpu.VMEM((total, width), F32),
+            pltpu.VMEM((nt * here // pieces, width), F32),
+        ],
+    )(smoothed.reshape(total, width), wi)
     return jnp.transpose(out.reshape(nt, here, 1, width), (1, 0, 2, 3))
 
 

time: 58.4 us -> 58.5 us (level)
  Pallas kernels: 56.1 us -> 58.3 us
  local copies, waits for them, and re-layouts: 2.12 us -> 0 us
    pallas_call x0 -> x1, Pallas kernels: none -> 3.4 us  [local(): pl.pallas_call(functools.partial(inverse_kernel, n_par, here), out_shape=...]
    unnamed x1 -> x0, local copies, waits for them, and re-layouts: 2.12 us -> none
    pallas_call x1, Pallas kernels: 56.1 us -> 54.9 us  [local(): pl.pallas_call(functools.partial(kernel, n_sens, n_par, probes, sensors,...]
where the time goes in v3:
time: 58.5 us; the launch traced here: 58.3 us
  Pallas kernels  58.3 us (100%)
    pallas_call x1, Pallas kernels, local(): pl.pallas_call(functools.partial(kernel, n_sens, n_par, probes, sensors,...  54.9 us
    pallas_call x1, Pallas kernels, local(): pl.pallas_call(functools.partial(inverse_kernel, n_par, here), out_shape=...  3.4 us

profile of v3, /device:TPU:0, one launch (start us, length us, event | category | flops | bytes accessed | tf_op | source)
XLA Modules:
  0.0 58.3 jit_solution(10415757664910585004)
XLA Ops:
  0.0 54.9 %shard_map.64 = (bf16[8,128,128]{2,1,0:T(8,128)(2,1)}, bf16[3,140,128]{2,1,0:T(8,128)(2,1)}) custom-call(bf16[3,1600,420]{2,1,0:T(8,128)(2,1)} %bitcast.12, bf16[8,2400,128]{2,1,0:T(8,128)(2,1)} %bitcast.13, s32[1,64]{1,0:T(1,128)} %bitcast.16, s32[1,150]{1,0:T(1,128)} %bitcast.15, f32[1,128]{1,0:T(1,128)} %kappa.1, f32[1,128]{1,0:T(1,128)} %theta.1), custom_call_target="tpu_custom_call" | custom-call | tf_op jit(solution)/shard_map/pallas_call | solution.py:434
  54.9 3.4 %shard_map.65 = bf16[3360,128]{1,0:T(8,128)(2,1)} custom-call(bf16[1024,128]{1,0:T(8,128)(2,1)} %bitcast.14, bf16[3,140,128]{2,1,0:T(8,128)(2,1)} %get-tuple-element.8.wi), custom_call_target="tpu_custom_call" | custom-call | tf_op jit(solution)/shard_map/pallas_call | solution.py:474

commit v4 on v3

--- a/solution.py
+++ b/solution.py
@@ -110,7 +110,6 @@
         load.start()
         loads.append(load)
     green_load = pltpu.make_async_copy(green_hbm, green_v, load_sem.at[chunks])
-    green_load.start()
 
     nt = wf.shape[0]
     nfreq = freqs.shape[1]
@@ -133,18 +132,8 @@
     add_rows = add_rows.astype(F32).astype(BF16)
     lane = iota((rows, wide), 1)
     keep = (lane % here == iota((rows, wide), 0) % here) & (lane < lanes)
-    for c in range(chunks):
-        loads[c].wait()
-        prod = jnp.dot(data_v[c], wf[...], preferred_element_type=F32)
-        prod = jnp.where(keep, prod, 0.0).astype(BF16)
-        sums = jnp.dot(add_rows, prod, preferred_element_type=F32)
-        for g in range(groups):
-            spec_f[g, c * sensors_chunk:(c + 1) * sensors_chunk, :] = sums[g * stack:g * stack + sensors_chunk]
-    ubuf[0, 0, spad - 16:, :] = jnp.zeros((16, groups * lanes), BF16)
-    for g in range(groups):
-        ubuf[0, 0, :sensors, g * lanes:(g + 1) * lanes] = spec_f[g][:, :lanes].astype(BF16)
-
-    pl.semaphore_wait(barrier, n_sens + n_par - 2)
+    marks = [(c * sensors_chunk) // 16 * 16 for c in range(chunks)] + [spad]
+    spec_f[:, spad - 16:, :] = jnp.zeros((groups, 16, wide), F32)
     sends = []
 
     def push(src, dst, ssem, rsem, peer):
@@ -162,32 +151,62 @@
     y_next = {"sens": ring_member((yring + 1) % ny, ny) * 2 + cpos}
     u_copies = {}
 
-    def gather_u(d):
+    def gather_u(d, c):
+        span = pl.ds(marks[c], marks[c + 1] - marks[c])
         if d:
-            u_copies[d, 0].wait_recv()
+            u_copies[d, 0, c].wait_recv()
         if d + 1 < ny:
-            u_copies[d + 1, 0] = push(ubuf.at[d, 0], ubuf.at[d + 1, 0], u_send.at[d, 0], u_recv.at[d + 1, 0], y_next)
-        u_copies[d, 1] = push(ubuf.at[d, 0], ubuf.at[d, 1], u_send.at[d, 1], u_recv.at[d, 1], core_peer)
-
-    gather_u(0)
+            u_copies[d + 1, 0, c] = push(
+                ubuf.at[d, 0, span], ubuf.at[d + 1, 0, span], u_send.at[d, 0, c], u_recv.at[d + 1, 0, c], y_next
+            )
+        u_copies[d, 1, c] = push(
+            ubuf.at[d, 0, span], ubuf.at[d, 1, span], u_send.at[d, 1, c], u_recv.at[d, 1, c], core_peer
+        )
+
+    for c in range(chunks):
+        loads[c].wait()
+        if c + 1 == chunks:
+            green_load.start()
+        prod = jnp.dot(data_v[c], wf[...], preferred_element_type=F32)
+        prod = jnp.where(keep, prod, 0.0).astype(BF16)
+        sums = jnp.dot(add_rows, prod, preferred_element_type=F32)
+        for g in range(groups):
+            spec_f[g, c * sensors_chunk:(c + 1) * sensors_chunk, :] = sums[g * stack:g * stack + sensors_chunk]
+        lo, hi = marks[c], marks[c + 1]
+        for g in range(groups):
+            ubuf[0, 0, lo:hi, g * lanes:(g + 1) * lanes] = spec_f[g, lo:hi, :][:, :lanes].astype(BF16)
+        if c == 0:
+            pl.semaphore_wait(barrier, n_sens + n_par - 2)
+        gather_u(0, c)
     c_copies = [push(coef.at[0], coef.at[e], c_send.at[e], c_recv.at[e], par_peer(e)) for e in range(1, n_par)]
 
-    green_load.wait()
     green_s[:, spad - 16:, :] = jnp.zeros((green_s.shape[0], 16, green_s.shape[2]), BF16)
 
-    def split(block, carry):
+    def split(block):
         green_f[...] = green_v[block].astype(F32)
         for k in range(kper):
             for c in range(2):
                 piece = green_f[pl.ds(k * 2 * sensors + c, sensors, stride=2), :]
                 green_s[block * kper + k, :sensors, c * width:(c + 1) * width] = piece.astype(BF16)
-        return carry
-
-    bounds = [n_par * d // ny for d in range(ny + 1)]
-    for d in range(ny):
-        if d:
-            gather_u(d)
-        lax.fori_loop(bounds[d], bounds[d + 1], split, 0)
+
+    steps = [(0, 0)]
+    for d in range(1, nz):
+        steps += [(d, 0), (d - 1, 1)]
+    steps.append((nz - 1, 1))
+
+    def owner(step):
+        d, xi = step
+        other = xpos if xi == 0 else 1 - xpos
+        return ring_member((zring - d + nz) % nz, nz) * 2 + other
+
+    ready = 0
+    green_load.wait()
+    for d in range(1, ny):
+        for c in range(chunks):
+            gather_u(d, c)
+            if c + 1 < chunks:
+                split(owner(steps[ready]))
+                ready += 1
 
     column = jnp.transpose(jnp.broadcast_to(order[...].astype(F32), (128, sensors)))[:, :1]
     wanted = jnp.broadcast_to(column, (sensors, spad))
@@ -196,7 +215,8 @@
     for d in range(ny):
         for ci in range(2):
             if ci:
-                u_copies[d, 1].wait_recv()
+                for c in range(chunks):
+                    u_copies[d, 1, c].wait_recv()
             source = ring_member((yring - d + ny) % ny, ny) * 2 + (cpos if ci == 0 else 1 - cpos)
             match = (wanted == (position + source * sensors).astype(F32)) & (position < sensors)
             picked = picked + jnp.dot(match.astype(F32).astype(BF16), ubuf[d, ci], preferred_element_type=F32)
@@ -209,15 +229,20 @@
     z_copies = {}
     x_copies = {}
 
+    halves = [pl.ds(0, cut)] + ([pl.ds(cut, spad - cut)] if cut < spad else [])
+
     def gather_v(d):
-        if d:
-            z_copies[d].wait_recv()
-        if d + 1 < nz:
-            z_copies[d + 1] = push(vbuf.at[d, 0], vbuf.at[d + 1, 0], z_send.at[d], z_recv.at[d + 1], z_next)
-        size = cut if d + 1 == nz else spad
-        x_copies[d] = push(
-            vbuf.at[d, 0, pl.ds(0, size)], vbuf.at[d, 1, pl.ds(0, size)], x_send.at[d], x_recv.at[d], partner
-        )
+        for p, span in enumerate(halves):
+            if d:
+                z_copies[d, p].wait_recv()
+            if d + 1 < nz:
+                z_copies[d + 1, p] = push(
+                    vbuf.at[d, 0, span], vbuf.at[d + 1, 0, span], z_send.at[d, p], z_recv.at[d + 1, p], z_next
+                )
+            if d + 1 < nz or p == 0:
+                x_copies[d, p] = push(
+                    vbuf.at[d, 0, span], vbuf.at[d, 1, span], x_send.at[d, p], x_recv.at[d, p], partner
+                )
 
     gather_v(0)
     freq_pair = iota((nfreq, 2 * nfreq), 0) == iota((nfreq, 2 * nfreq), 1) // 2
@@ -228,27 +253,18 @@
 
     rs_copies = {}
     a_copies = []
-    steps = [(0, 0)]
-    for d in range(1, nz):
-        steps += [(d, 0), (d - 1, 1)]
-    steps.append((nz - 1, 1))
-
-    def owner(step):
-        d, xi = step
-        other = xpos if xi == 0 else 1 - xpos
-        return ring_member((zring - d + nz) % nz, nz) * 2 + other
-
     def products(index):
         d, xi = steps[index]
         if xi:
-            x_copies[d].wait_recv()
-            if d + 2 == nz and cut < spad:
-                rest = pl.ds(cut, spad - cut)
-                z_copies[nz] = push(
-                    vbuf.at[d, 1, rest], vbuf.at[d + 1, 1, rest], z_send.at[nz], z_recv.at[nz], z_next
-                )
-            if d + 1 == nz and cut < spad:
-                z_copies[nz].wait_recv()
+            for p, span in enumerate(halves):
+                if (d, p) in x_copies:
+                    x_copies[d, p].wait_recv()
+                if d + 2 == nz and p == 1:
+                    z_copies[nz, 1] = push(
+                        vbuf.at[d, 1, span], vbuf.at[d + 1, 1, span], z_send.at[nz, 1], z_recv.at[nz, 1], z_next
+                    )
+                if d + 1 == nz and p == 1:
+                    z_copies[nz, 1].wait_recv()
         elif d:
             gather_v(d)
         block = owner(steps[index])
@@ -288,6 +304,8 @@
             )
 
     for index in range(n_par):
+        if index >= ready:
+            split(owner(steps[index]))
         products(index)
         if index >= 2:
             reduce(index - 2)
@@ -445,7 +463,7 @@
             pltpu.VMEM(blocks.shape, BF16),
             pltpu.VMEM(blocks.shape[1:], F32),
             pltpu.VMEM((nfreq, spad, 2 * cells), BF16),
-            pltpu.VMEM((n_sens, sensors, wide), F32),
+            pltpu.VMEM((n_sens, spad, wide), F32),
             pltpu.VMEM((n_sens // 2, 2, spad, n_sens * lanes), BF16),
             pltpu.VMEM((nz, 2, spad, n_sens * lanes), BF16),
             pltpu.VMEM((n_sens * lanes, spad), BF16),
@@ -458,9 +476,9 @@
             pltpu.VMEM((n_par, block, width), BF16),
             pltpu.VMEM((n_par * block, width), F32),
             dma((chunks + 1,)),
-            dma((n_sens // 2, 2)), dma((n_sens // 2, 2)),
-            dma((nz + 1,)), dma((nz + 1,)),
-            dma((nz,)), dma((nz,)),
+            dma((n_sens // 2, 2, chunks)), dma((n_sens // 2, 2, chunks)),
+            dma((nz + 1, 2)), dma((nz + 1, 2)),
+            dma((nz, 2)), dma((nz, 2)),
             dma((n_par, n_sens - 1)), dma((n_par, n_sens - 1)),
             dma((n_par,)), dma((n_par,)),
             dma((n_par,)), dma((n_par,)),

time: 58.5 us -> 55.7 us (0.952)
  Pallas kernels: 58.3 us -> 55.4 us
    pallas_call x1, Pallas kernels: 54.9 us -> 52 us  [local(): pl.pallas_call(functools.partial(kernel, n_sens, n_par, probes, sensors,...]
where the time goes in v4:
time: 55.7 us; the launch traced here: 55.4 us
  Pallas kernels  55.4 us (99%)
    pallas_call x1, Pallas kernels, local(): pl.pallas_call(functools.partial(kernel, n_sens, n_par, probes, sensors,...  52 us
    pallas_call x1, Pallas kernels, local(): pl.pallas_call(functools.partial(inverse_kernel, n_par, here), out_shape=...  3.38 us

profile of v4, /device:TPU:0, one launch (start us, length us, event | category | flops | bytes accessed | tf_op | source)
XLA Modules:
  0.0 55.4 jit_solution(8459670918251910168)
XLA Ops:
  0.0 52.0 %shard_map.64 = (bf16[8,128,128]{2,1,0:T(8,128)(2,1)}, bf16[3,140,128]{2,1,0:T(8,128)(2,1)}) custom-call(bf16[3,1600,420]{2,1,0:T(8,128)(2,1)} %bitcast.12, bf16[8,2400,128]{2,1,0:T(8,128)(2,1)} %bitcast.13, s32[1,64]{1,0:T(1,128)} %bitcast.16, s32[1,150]{1,0:T(1,128)} %bitcast.15, f32[1,128]{1,0:T(1,128)} %kappa.1, f32[1,128]{1,0:T(1,128)} %theta.1), custom_call_target="tpu_custom_call" | custom-call | tf_op jit(solution)/shard_map/pallas_call | solution.py:452
  52.0 3.4 %shard_map.65 = bf16[3360,128]{1,0:T(8,128)(2,1)} custom-call(bf16[1024,128]{1,0:T(8,128)(2,1)} %bitcast.14, bf16[3,140,128]{2,1,0:T(8,128)(2,1)} %get-tuple-element.8.wi), custom_call_target="tpu_custom_call" | custom-call | tf_op jit(solution)/shard_map/pallas_call | solution.py:492

commit v5 on v4

--- a/solution.py
+++ b/solution.py
@@ -116,7 +116,7 @@
     freq_rows = jnp.broadcast_to(freqs[...], (8, nfreq)).astype(F32).astype(BF16)
     wide = wf.shape[1]
     chosen = iota((nfreq, wide), 0) == b * kper + iota((nfreq, wide), 1) // (2 * here)
-    wf[...] = table(freq_rows, chosen.astype(F32).astype(BF16), iota((nt, wide), 1) // here % 2, nt, nt)
+    wf[...] = table(freq_rows, chosen.astype(F32).astype(BF16), iota((1, wide), 1) // here % 2, nt, nt)
 
     pick = (iota((width, width), 0) // n_par + b * cg == iota((width, width), 1)).astype(F32)
     own = iota((n_par, width), 1) % n_par == iota((n_par, width), 0)
@@ -127,11 +127,14 @@
     rows = data_v.shape[1]
     sensors_chunk = sensors // chunks
     stack = round_up(sensors_chunk, 8)
-    qshape = (groups * stack, rows)
-    add_rows = iota(qshape, 1) // here == iota(qshape, 0) % stack * groups + iota(qshape, 0) // stack
+    pile = groups * stack
+    place = iota((pile, 1), 0)
+    place = place % stack * groups + place // stack
+    group_of = iota((1, rows), 1) // here
+    add_rows = jnp.broadcast_to(place, (pile, rows)) == jnp.broadcast_to(group_of, (pile, rows))
     add_rows = add_rows.astype(F32).astype(BF16)
-    lane = iota((rows, wide), 1)
-    keep = (lane % here == iota((rows, wide), 0) % here) & (lane < lanes)
+    lane = iota((1, here, wide), 2)
+    keep = (lane % here == iota((1, here, wide), 1)) & (lane < lanes)
     marks = [(c * sensors_chunk) // 16 * 16 for c in range(chunks)] + [spad]
     spec_f[:, spad - 16:, :] = jnp.zeros((groups, 16, wide), F32)
     sends = []
@@ -168,7 +171,7 @@
         if c + 1 == chunks:
             green_load.start()
         prod = jnp.dot(data_v[c], wf[...], preferred_element_type=F32)
-        prod = jnp.where(keep, prod, 0.0).astype(BF16)
+        prod = jnp.where(keep, prod.reshape(rows // here, here, wide), 0.0).reshape(rows, wide).astype(BF16)
         sums = jnp.dot(add_rows, prod, preferred_element_type=F32)
         for g in range(groups):
             spec_f[g, c * sensors_chunk:(c + 1) * sensors_chunk, :] = sums[g * stack:g * stack + sensors_chunk]
@@ -246,13 +249,14 @@
 
     gather_v(0)
     freq_pair = iota((nfreq, 2 * nfreq), 0) == iota((nfreq, 2 * nfreq), 1) // 2
-    wi = table(freq_rows, freq_pair.astype(F32).astype(BF16), iota((nt, 2 * nfreq), 1) % 2, nt, nfreq)
+    wi = table(freq_rows, freq_pair.astype(F32).astype(BF16), iota((1, 2 * nfreq), 1) % 2, nt, nfreq)
     steps_here = wi_out.shape[1]
     for p in range(wi_out.shape[0]):
         wi_out[p] = wi[p * steps_here:(p + 1) * steps_here]
 
     rs_copies = {}
     a_copies = []
+
     def products(index):
         d, xi = steps[index]
         if xi:
@@ -412,21 +416,23 @@
         copy.wait_send()
 
 
-def inverse_kernel(n_par, here, smoothed, wi, out, sf, tall):
+def inverse_kernel(n_par, here, smoothed, wi, out, sf, ordered, tall):
     width = out.shape[1]
     cg = width // n_par
     fields = smoothed.shape[0]
 
     @pl.when(pl.program_id(0) == 0)
     def _():
-        source = iota((width, width), 0)
-        perm = ((source % cg) * n_par + source // cg == iota((width, width), 1)).astype(F32).astype(BF16)
-        sf[...] = jnp.dot(smoothed[...], perm, preferred_element_type=F32)
+        source = iota((width, 1), 0)
+        target = source % cg * n_par + source // cg
+        perm = jnp.broadcast_to(target, (width, width)) == iota((width, width), 1)
+        sf[...] = jnp.dot(smoothed[...], perm.astype(F32).astype(BF16), preferred_element_type=F32)
+        for r in range(here):
+            ordered[r] = sf[pl.ds(r, fields // here, stride=here), :].astype(BF16)
 
     steps = tall.shape[0] // here
     for r in range(here):
-        mine = sf[pl.ds(r, fields // here, stride=here), :].astype(BF16)
-        tall[pl.ds(r, steps, stride=here), :] = jnp.dot(wi[0], mine, preferred_element_type=F32)
+        tall[pl.ds(r, steps, stride=here), :] = jnp.dot(wi[0], ordered[r], preferred_element_type=F32)
     out[...] = tall[...].astype(BF16)
 
 
@@ -500,6 +506,7 @@
         out_specs=pl.BlockSpec((nt * here // pieces, width), lambda i: (i, 0)),
         scratch_shapes=[
             pltpu.VMEM((total, width), F32),
+            pltpu.VMEM((here, total // here, width), BF16),
             pltpu.VMEM((nt * here // pieces, width), F32),
         ],
     )(smoothed.reshape(total, width), wi)

time: 55.7 us -> 55.7 us (level)
  no operation moved by 1% of the time
where the time goes in v5:
time: 55.7 us; the launch traced here: 55.5 us
  Pallas kernels  55.4 us (99%)
    pallas_call x1, Pallas kernels, local(): pl.pallas_call(functools.partial(kernel, n_sens, n_par, probes, sensors,...  52 us
    pallas_call x1, Pallas kernels, local(): pl.pallas_call(functools.partial(inverse_kernel, n_par, here), out_shape=...  3.42 us

profile of v5, /device:TPU:0, one launch (start us, length us, event | category | flops | bytes accessed | tf_op | source)
XLA Modules:
  0.0 55.5 jit_solution(17141251673856064931)
XLA Ops:
  0.0 52.0 %shard_map.64 = (bf16[8,128,128]{2,1,0:T(8,128)(2,1)}, bf16[3,140,128]{2,1,0:T(8,128)(2,1)}) custom-call(bf16[3,1600,420]{2,1,0:T(8,128)(2,1)} %bitcast.12, bf16[8,2400,128]{2,1,0:T(8,128)(2,1)} %bitcast.13, s32[1,64]{1,0:T(1,128)} %bitcast.16, s32[1,150]{1,0:T(1,128)} %bitcast.15, f32[1,128]{1,0:T(1,128)} %kappa.1, f32[1,128]{1,0:T(1,128)} %theta.1), custom_call_target="tpu_custom_call" | custom-call | tf_op jit(solution)/shard_map/pallas_call | solution.py:458
  52.0 3.4 %shard_map.65 = bf16[3360,128]{1,0:T(8,128)(2,1)} custom-call(bf16[1024,128]{1,0:T(8,128)(2,1)} %bitcast.14, bf16[3,140,128]{2,1,0:T(8,128)(2,1)} %get-tuple-element.8.wi), custom_call_target="tpu_custom_call" | custom-call | tf_op jit(solution)/shard_map/pallas_call | solution.py:498

commit v6 on v5

--- a/solution.py
+++ b/solution.py
@@ -395,9 +395,10 @@
             ysend[i, pl.ds(start, tile), :] = both.astype(BF16)
         return carry
 
-    cuts = [0, fields // tile // 2, fields // tile]
+    parts = y_send.shape[0]
+    cuts = [fields // tile * i // parts for i in range(parts + 1)]
     y_copies = []
-    for half in range(2):
+    for half in range(parts):
         lax.fori_loop(cuts[half], cuts[half + 1], smooth, 0)
         span = pl.ds(cuts[half] * tile, (cuts[half + 1] - cuts[half]) * tile)
         for e in range(1, n_par):
@@ -488,7 +489,7 @@
             dma((n_par, n_sens - 1)), dma((n_par, n_sens - 1)),
             dma((n_par,)), dma((n_par,)),
             dma((n_par,)), dma((n_par,)),
-            dma((2, n_par)), dma((2, n_par)),
+            dma((min(4, block // 16), n_par)), dma((min(4, block // 16), n_par)),
         ],
         compiler_params=pltpu.CompilerParams(
             collective_id=0, has_side_effects=True, vmem_limit_bytes=56 * 1024 * 1024

time: 55.7 us -> 55.3 us (level)
  no operation moved by 1% of the time
where the time goes in v6:
time: 55.3 us; the launch traced here: 55.1 us
  Pallas kernels  55 us (99%)
    pallas_call x1, Pallas kernels, local(): pl.pallas_call(functools.partial(kernel, n_sens, n_par, probes, sensors,...  51.6 us
    pallas_call x1, Pallas kernels, local(): pl.pallas_call(functools.partial(inverse_kernel, n_par, here), out_shape=...  3.41 us

profile of v6, /device:TPU:0, one launch (start us, length us, event | category | flops | bytes accessed | tf_op | source)
XLA Modules:
  0.0 55.1 jit_solution(6361252020169270753)
XLA Ops:
  0.0 51.6 %shard_map.64 = (bf16[8,128,128]{2,1,0:T(8,128)(2,1)}, bf16[3,140,128]{2,1,0:T(8,128)(2,1)}) custom-call(bf16[3,1600,420]{2,1,0:T(8,128)(2,1)} %bitcast.12, bf16[8,2400,128]{2,1,0:T(8,128)(2,1)} %bitcast.13, s32[1,64]{1,0:T(1,128)} %bitcast.16, s32[1,150]{1,0:T(1,128)} %bitcast.15, f32[1,128]{1,0:T(1,128)} %kappa.1, f32[1,128]{1,0:T(1,128)} %theta.1), custom_call_target="tpu_custom_call" | custom-call | tf_op jit(solution)/shard_map/pallas_call | solution.py:459
  51.6 3.4 %shard_map.65 = bf16[3360,128]{1,0:T(8,128)(2,1)} custom-call(bf16[1024,128]{1,0:T(8,128)(2,1)} %bitcast.14, bf16[3,140,128]{2,1,0:T(8,128)(2,1)} %get-tuple-element.8.wi), custom_call_target="tpu_custom_call" | custom-call | tf_op jit(solution)/shard_map/pallas_call | solution.py:499

commit v7 on v6

--- a/solution.py
+++ b/solution.py
@@ -448,7 +448,7 @@
     spad = round_up(sensors, 16)
     wide = round_up(lanes, 128)
     chunks = 3
-    pieces = 3
+    pieces = 1
     flat = jnp.transpose(data, (1, 0, 2)).reshape(chunks, sensors * probes // chunks, nt)
     blocks = green.reshape(n_par, kper * sensors * 2, cells)
     vmem = pl.BlockSpec(memory_space=pltpu.VMEM)

time: 55.3 us -> 54.7 us (0.989)
  no operation moved by 1% of the time
where the time goes in v7:
time: 54.7 us; the launch traced here: 54.5 us
  Pallas kernels  54.5 us (100%)
    pallas_call x1, Pallas kernels, local(): pl.pallas_call(functools.partial(kernel, n_sens, n_par, probes, sensors,...  51.6 us
    pallas_call x1, Pallas kernels, local(): pl.pallas_call(functools.partial(inverse_kernel, n_par, here), out_shape=...  2.91 us

profile of v7, /device:TPU:0, one launch (start us, length us, event | category | flops | bytes accessed | tf_op | source)
XLA Modules:
  0.0 54.5 jit_solution(4126507110672715564)
XLA Ops:
  0.0 51.6 %shard_map.64 = (bf16[8,128,128]{2,1,0:T(8,128)(2,1)}, bf16[1,420,128]{2,1,0:T(8,128)(2,1)}) custom-call(bf16[3,1600,420]{2,1,0:T(8,128)(2,1)} %bitcast.12, bf16[8,2400,128]{2,1,0:T(8,128)(2,1)} %bitcast.13, s32[1,64]{1,0:T(1,128)} %bitcast.16, s32[1,150]{1,0:T(1,128)} %bitcast.15, f32[1,128]{1,0:T(1,128)} %kappa.1, f32[1,128]{1,0:T(1,128)} %theta.1), custom_call_target="tpu_custom_call" | custom-call | tf_op jit(solution)/shard_map/pallas_call | solution.py:459
  51.6 2.9 %shard_map.65 = bf16[3360,128]{1,0:T(8,128)(2,1)} custom-call(bf16[1024,128]{1,0:T(8,128)(2,1)} %bitcast.14, bf16[1,420,128]{2,1,0:T(8,128)(2,1)} %get-tuple-element.8.wi), custom_call_target="tpu_custom_call" | custom-call | tf_op jit(solution)/shard_map/pallas_call | solution.py:499
